TPU v7x, 512 devices: a whole 4x4x16 slice. The times are simulated.
512 devices in a mesh: chan: 64 (over x, z), tm: 8 (over y, core).
Axes of the slice: x: 4, y: 4, z: 16, core: 2. Of those that a mesh axis runs over, the one named last changes fastest.
Arguments:
- voltages: float32 [512, 3072, 128], P('chan', 'tm'), may hold values from -11 to 11
- steering: int32 [64, 512, 512], P('chan'), may hold values from 0 to 1023
- chirp_phase: float32 [64, 512], P('chan'), may hold values from -3.140625 to 3.140625
- delays: int32 [1, 64], replicated, may hold values from 0 to 383
Outputs:
- trial_spectra: float32 [512, 1, 2, 1024], P('chan', None, None, 'tm')
All inputs are finite; a program needn't handle non-finite values.
Results may differ from a plain program's by a relative error of at most 0.00012.
Values sent between devices are 32-bit elements; how exact they have to be, the bound alone decides.
A program may use at most 64 MiB of HBM per device.

v0:
```python
import math

import jax
import jax.numpy as jnp
from jax import lax
from jax.sharding import PartitionSpec as P

HALO = 128
FREQ = 128
PHASES = 1024


exact_arithmetic = lax.Precision.HIGHEST
epsilon = 1e-06


def from_behind(value, axis, steps):
    count = lax.axis_size(axis)
    initial, last = (max(0, -steps), min(count, count - steps))
    return lax.ppermute(value, axis, [(source, source + steps) for source in range(initial, last)])


def angle_tables(row_count, col_count, length, col_first):
    row_index = jnp.arange(row_count, dtype=jnp.int32)[:, None]
    col_index = jnp.arange(col_count, dtype=jnp.int32)[None, :] + col_first
    turn_count = row_index * col_index % length
    angles = turn_count.astype(jnp.float32) * (2.0 * math.pi / length)
    return (jnp.cos(angles), jnp.sin(angles))


def channel_table(channels):
    cos_part, sin_part = angle_tables(channels, channels, channels, 0)
    upper_rows = jnp.stack([cos_part, -sin_part], axis=1)
    lower_rows = jnp.stack([sin_part, cos_part], axis=1)
    return jnp.concatenate([upper_rows, lower_rows], axis=0) / math.sqrt(channels)


def steer_matrix(phase_rows, stations):
    angles = phase_rows.astype(jnp.float32) * (2.0 * math.pi / PHASES)
    weight_real = jnp.cos(angles)
    weight_imag = jnp.sin(angles)
    upper_rows = jnp.concatenate([weight_real, -weight_imag], axis=1)
    lower_rows = jnp.concatenate([weight_imag, weight_real], axis=1)
    return jnp.concatenate([upper_rows, lower_rows], axis=0) / math.sqrt(stations)


def forward_matrix(window):
    cos_part, sin_part = angle_tables(window, window, window, 0)
    upper_rows = jnp.concatenate([cos_part, -sin_part], axis=1)
    lower_rows = jnp.concatenate([sin_part, cos_part], axis=1)
    return jnp.concatenate([upper_rows, lower_rows], axis=0)


def inverse_matrix(window, block_len, halo_len):
    cos_part, sin_part = angle_tables(window, block_len, window, halo_len)
    upper_rows = jnp.concatenate([cos_part, sin_part], axis=1)
    lower_rows = jnp.concatenate([-sin_part, cos_part], axis=1)
    return jnp.concatenate([upper_rows, lower_rows], axis=0) / window


def block_matrix(block_len, bin_count):
    cos_part, sin_part = angle_tables(block_len, bin_count, block_len, 1)
    return jnp.concatenate([cos_part, -sin_part], axis=1) / math.sqrt(block_len)


def dedisperse(window_flat, chirp_row, forward_table, inverse_table, block_len):
    window = chirp_row.shape[0]
    spectrum = jnp.dot(window_flat, forward_table, precision=exact_arithmetic)
    spectrum_real = spectrum[:, :window]
    spectrum_imag = spectrum[:, window:]
    chirp_cos = jnp.cos(chirp_row)[None, :]
    chirp_sin = jnp.sin(chirp_row)[None, :]
    shifted_real = spectrum_real * chirp_cos - spectrum_imag * chirp_sin
    shifted_imag = spectrum_real * chirp_sin + spectrum_imag * chirp_cos
    restored = jnp.dot(
        jnp.concatenate([shifted_real, shifted_imag], axis=1),
        inverse_table,
        precision=exact_arithmetic,
    )
    return restored[:, :block_len] ** 2 + restored[:, block_len:] ** 2


def trial_sum(normed, delay_rows, block_table, block_len, channels):
    bin_count = block_table.shape[1] // 2
    spectra = jnp.einsum("cbt,tg->cbg", normed, block_table, precision=exact_arithmetic)
    frequency_real_values = spectra[:, :, :bin_count]
    frequency_imaginary_values = spectra[:, :, bin_count:]
    bin_index = jnp.arange(1, bin_count + 1, dtype=jnp.int32)
    turn_count = delay_rows[:, :, None] * bin_index[None, None, :] % block_len
    angles = turn_count.astype(jnp.float32) * (2.0 * math.pi / block_len)
    phase_shift_cosine = jnp.cos(angles)
    phase_shift_sine = jnp.sin(angles)
    real_component = jnp.einsum(
        "ope,roe->pre", frequency_real_values, phase_shift_cosine, precision=exact_arithmetic
    ) - jnp.einsum(
        "ope,roe->pre", frequency_imaginary_values, phase_shift_sine, precision=exact_arithmetic
    )
    imaginary_component = jnp.einsum(
        "ope,roe->pre", frequency_real_values, phase_shift_sine, precision=exact_arithmetic
    ) + jnp.einsum(
        "ope,roe->pre", frequency_imaginary_values, phase_shift_cosine, precision=exact_arithmetic
    )
    return jnp.stack([real_component, imaginary_component], axis=2) / math.sqrt(channels)


def local(voltages, steering, chirp_phase, delays):
    chan_local = steering.shape[0]
    beam_count = steering.shape[1]
    stations = steering.shape[2]
    block_len = voltages.shape[1]
    channels = voltages.shape[2] // 2
    window = block_len + HALO
    split = jnp.einsum(
        "stn,nqc->cqst", voltages, channel_table(channels), precision=exact_arithmetic
    )
    turned = lax.all_to_all(split, "chan", split_axis=0, concat_axis=2, tiled=True)
    forward_table = forward_matrix(window)
    inverse_table = inverse_matrix(window, block_len, HALO)
    stacked = turned[0].reshape(2 * stations, turned.shape[3])
    formed = jnp.dot(steer_matrix(steering[0], stations), stacked, precision=exact_arithmetic)
    earlier_beams = from_behind(formed[:, block_len - HALO :], "tm", 1)
    window_rows = jnp.concatenate([earlier_beams, formed], axis=1)
    window_flat = jnp.concatenate([window_rows[:beam_count], window_rows[beam_count:]], axis=1)
    detected_rows = [
        dedisperse(window_flat, chirp_phase[0], forward_table, inverse_table, block_len)
    ]
    detected = jnp.stack(detected_rows, axis=0)
    spectra_all = block_len * lax.axis_size("tm")
    mean_power = lax.psum(jnp.sum(detected, axis=2), "tm") / spectra_all
    centred = detected - mean_power[:, :, None]
    spread = lax.psum(jnp.sum(centred * centred, axis=2), "tm") / spectra_all
    normed = centred * lax.rsqrt(spread + epsilon)[:, :, None]
    block_table = block_matrix(block_len, FREQ)
    own_delays = lax.dynamic_slice_in_dim(
        delays, lax.axis_index("chan") * chan_local, chan_local, 1
    )
    return lax.psum_scatter(
        trial_sum(normed, own_delays, block_table, block_len, channels),
        "chan",
        scatter_dimension=0,
        tiled=True,
    )


def solution(mesh):
    in_specs = (P("chan", "tm", None), P("chan", None, None), P("chan", None), P())
    out_specs = P("chan", None, None, "tm")
    return jax.shard_map(local, mesh=mesh, in_specs=in_specs, out_specs=out_specs, check_vma=False)
```

profile of v0, /device:TPU:1, one launch (start us, length us, event | category | flops | bytes accessed | tf_op | source)
XLA Modules:
  0.0 633.8 jit_solution(991689627475474)
XLA Ops:
  6.5 0.0 copy-start
  6.5 0.1 fusion.84
  6.7 0.1 fusion.86
  6.8 1.1 copy-done
  7.9 1.5 fusion.33
  9.5 2.1 copy.8
  11.5 0.0 copy-start.9
  11.5 19.2 %all-to-all-start = ((f32[64,2,8,384]{3,2,1,0:T(8,128)}), f32[64,2,8,384]{3,2,1,0:T(8,128)S(1)}, u32[]{:S(2)}, u32[]{:S(2)}) async-start(f32[64,2,8,384]{3,2,1,0:T(8,128)} %copy.8), calls=%async_computation | async-start | bytes 3145728 | tf_op jit(solution)/shard_map/all_to_all | solution.py:116
  30.8 0.0 copy-start.8
  30.8 0.2 reduce-scatter.2.cloned.1.call-start
  31.0 0.0 copy-done.9
  31.0 0.0 copy-start.1
  31.1 0.6 constant_dynamic-slice_fusion
  31.6 1.3 fusion.89
  32.9 4.6 fusion.54
  37.6 5.0 fusion.52
  42.5 0.0 copy-done.8
  42.5 0.1 fusion.103
  42.6 0.0 copy-done.1
  42.6 4.3 fusion.100
  46.9 4.6 sine_bitcast_fusion
  51.5 49.6 %all-to-all-done = f32[64,2,8,384]{3,2,1,0:T(8,128)S(1)} async-done(((f32[64,2,8,384]{3,2,1,0:T(8,128)}), f32[64,2,8,384]{3,2,1,0:T(8,128)S(1)}, u32[]{:S(2)}, u32[]{:S(2)}) %all-to-all-start) | async-done | bytes 1572896 | tf_op jit(solution)/shard_map/all_to_all | solution.py:116
  101.1 0.0 copy-start.2
  101.1 0.0 copy-start.3
  101.1 0.0 copy-start.7
  101.1 0.1 copy.9
  101.2 1.1 copy-done.2
  102.3 0.3 copy-done.3
  102.7 0.3 copy-done.7
  103.0 5.4 fusion
  108.4 10.1 %collective-permute-start = (f32[1024,128]{0,1:T(8,128)S(1)}, f32[1024,128]{0,1:T(8,128)S(1)}, u32[]{:S(2)}, u32[]{:S(2)}) collective-permute-start(f32[1024,128]{0,1:T(8,128)S(1)} %slice.36), channel_id=1, source_target_pairs={{0,1},{1,2},{2,3},{3,4},{4,5},{5,6},{6,7},{8,9},{9,10},{10,11},{11... | collective-permute-start | bytes 1572872 | tf_op jit(solution)/shard_map/ppermute | solution.py:20
  118.5 0.8 fusion.67
  119.3 3.1 fusion.59
  122.4 0.0 copy-start.4
  122.4 0.0 copy-start.5
  122.4 0.0 copy-start.6
  122.5 1.9 collective-permute-done
  124.4 0.1 fusion.39
  124.5 0.0 copy-done.4
  124.5 0.0 copy-done.5
  124.5 0.0 copy-done.6
  124.5 6.8 %fusion.7 = f32[512,1024]{1,0:T(8,128)S(1)} fusion(f32[512,512]{1,0:T(8,128)S(1)} %copy-done.6, f32[512,512]{1,0:T(8,128)S(1)} %copy-done.5, f32[512,512]{1,0:T(8,128)S(1)} %copy-done.4, f32[1024,384]{0,1:T(8,128)S(1)} %fusion, f32[1024,128]{0,1:T(8,128)S(1)} %collective-permute-done, f32[512,512]{0,1:T(8,128)S(1)} %fusion.39), kind=kOutput, calls=%fused_computation.8 | convolution fusion | flops 6446645248 | bytes 8388608 | tf_op jit(solution)/shard_map/dot_general | solution.py:68
  131.3 0.3 multiply_subtract_fusion
  131.6 5.6 fusion.15
  137.2 0.2 fusion.102
  137.4 13.2 %psum.14 = f32[1,512]{1,0:T(1,128)S(1)} all-reduce(f32[1,512]{1,0:T(1,128)S(1)} %bitcast.66), channel_id=1, replica_groups=mesh['chan'=64,'tm'=8] {'tm'}, use_global_device_ids=true, to_apply=%region_1.2 | all-reduce | flops 512 | bytes 4096 | tf_op jit(solution)/shard_map/psum | solution.py:129
  150.6 0.2 multiply_reduce_fusion
  150.9 11.9 %psum.15 = f32[1,512]{1,0:T(1,128)S(1)} all-reduce(f32[1,512]{1,0:T(1,128)S(1)} %bitcast.67), channel_id=1, replica_groups=mesh['chan'=64,'tm'=8] {'tm'}, use_global_device_ids=true, to_apply=%region_3.4 | all-reduce | flops 512 | bytes 4096 | tf_op jit(solution)/shard_map/psum | solution.py:131
  162.8 1.1 convolution_bitcast_fusion
  164.0 0.7 subtract_bitcast_fusion
  164.7 0.8 maximum_multiply_fusion.4
  165.5 0.0 reduce-scatter.2.cloned.1.call-update
  165.5 460.1 %reduce-scatter.2.cloned.1.call-done = f32[8,1,2,128]{3,0,2,1:T(8,128)} async-done(((f32[512,1,2,128]{3,0,2,1:T(8,128)}), f32[8,1,2,128]{3,0,2,1:T(8,128)}) %reduce-scatter.2.cloned.1.call-update) | async-done | bytes 8208 | tf_op jit(solution)/shard_map/reduce_scatter | solution.py:137
  625.7 1.3 copy.10
  (5 shorter events, 0.1 us)
Async XLA Ops:
  6.5 1.4 copy-start
  11.5 19.5 %copy-start.9 = (s32[1,64]{1,0:T(1,128)S(1)}, s32[1,64]{1,0:T(1,128)}, u32[]{:S(2)}) copy-start(s32[1,64]{1,0:T(1,128)} %param.7) | copy-start | bytes 772
  11.5 89.6 %all-to-all-start = ((f32[64,2,8,384]{3,2,1,0:T(8,128)}), f32[64,2,8,384]{3,2,1,0:T(8,128)S(1)}, u32[]{:S(2)}, u32[]{:S(2)}) async-start(f32[64,2,8,384]{3,2,1,0:T(8,128)} %copy.8), calls=%async_computation | async-start | bytes 3145728 | tf_op jit(solution)/shard_map/all_to_all | solution.py:116
  30.8 11.7 %copy-start.8 = (f32[1,512]{1,0:T(1,128)S(1)}, f32[1,512]{1,0:T(1,128)}, u32[]{:S(2)}) copy-start(f32[1,512]{1,0:T(1,128)} %param.6) | copy-start | bytes 6148
  30.8 594.9 %reduce-scatter.2.cloned.1.call-start = ((), (), s32[]{:S(2)}) async-start(), calls=%async_computation.2 | async-start | bytes 532480 | tf_op jit(solution)/shard_map/reduce_scatter | solution.py:137
  31.0 11.6 %copy-start.1 = (s32[1,512,512]{2,1,0:T(8,128)S(1)}, s32[1,512,512]{2,1,0:T(8,128)}, u32[]{:S(2)}) copy-start(s32[1,512,512]{2,1,0:T(8,128)} %param.5) | copy-start | bytes 3145732
  101.1 1.2 copy-start.2
  101.1 1.5 copy-start.3
  101.1 1.9 copy-start.7
  108.4 16.0 %collective-permute-start = (f32[1024,128]{0,1:T(8,128)S(1)}, f32[1024,128]{0,1:T(8,128)S(1)}, u32[]{:S(2)}, u32[]{:S(2)}) collective-permute-start(f32[1024,128]{0,1:T(8,128)S(1)} %slice.36), channel_id=1, source_target_pairs={{0,1},{1,2},{2,3},{3,4},{4,5},{5,6},{6,7},{8,9},{9,10},{10,11},{11... | collective-permute-start | bytes 1572872 | tf_op jit(solution)/shard_map/ppermute | solution.py:20
  122.4 2.0 copy-start.4
  122.4 2.0 copy-start.5
  122.4 2.0 copy-start.6
Sparse Core Ops, SparseCore 0:
  165.7 459.9 reduce-scatter.1
where the time goes:
time: 645 us; the launch traced here: 634 us
  waiting for transfers between devices  512 us (79%)
  starting transfers between devices  29.5 us (5%)
  other arithmetic  26.4 us (4%)
  blocking collectives  25.2 us (4%)
  matrix products  20.4 us (3%)
  between operations  13.6 us (2%)
  local copies, waits for them, and re-layouts  7.06 us (1%)
    reduce_scatter x1, waiting for transfers between devices, local(): lax.psum_scatter(trial_sum(normed, own_delays, block_table, block_len, ch...  460 us
    all_to_all x1, waiting for transfers between devices, local(): lax.all_to_all(split, 'chan', split_axis=0, concat_axis=2, tiled=True)  49.6 us
    all_to_all x1, starting transfers between devices, local(): lax.all_to_all(split, 'chan', split_axis=0, concat_axis=2, tiled=True)  19.2 us
    psum x1, blocking collectives, local(): mean_power = lax.psum(jnp.sum(detected, axis=2), 'tm') / spectra_all  13.2 us
  transfers between devices with their start and end apart: 3, of which 3 were waited for; matrix products, arithmetic and copies ran while one was open for 4% of the time, Pallas kernels for 0%

commit v1 on v0

v1 whole, which is shorter than its diff:
```python
import math

import jax
import jax.numpy as jnp
from jax import lax
from jax.experimental import pallas as pl
from jax.experimental.pallas import tpu as pltpu
from jax.sharding import PartitionSpec as P

MESH = pl.DeviceIdType.MESH
F32 = jnp.float32
BF16 = jnp.bfloat16

NX, NZ, NT = 4, 16, 8
NC = NX * NZ
BEAMS = 512
STATIONS = 512
PER = STATIONS // NC
ROWS = 2 * PER
CHANNELS = 64
BLOCK = 384
HALO = 128
WINDOW = 512
FREQ = 128
PHASES = 1024
SPECTRA = 3072
T = 128
PARTS = BLOCK // T
SLABS = 2
SB = BEAMS // SLABS
EPSILON = 1e-06
THIRD = (2, 0, 1)


def sincos(turns, period):
    quarter = ((turns + period / 8) * (4.0 / period)).astype(jnp.int32)
    t = (turns - quarter.astype(F32) * (period / 4)) * (2.0 * math.pi / period)
    t2 = t * t
    s = t * (1.0 + t2 * (-1 / 6 + t2 * (1 / 120 + t2 * (-1 / 5040 + t2 * (1 / 362880)))))
    c = 1.0 + t2 * (-1 / 2 + t2 * (1 / 24 + t2 * (-1 / 720 + t2 * (1 / 40320 - t2 * (1 / 3628800)))))
    odd = (quarter & 1) == 1
    cos_part = jnp.where(odd, s, c)
    sin_part = jnp.where(odd, c, s)
    cos_part = jnp.where(((quarter + 1) & 2) == 2, -cos_part, cos_part)
    sin_part = jnp.where((quarter & 2) == 2, -sin_part, sin_part)
    return cos_part, sin_part


def modulo(value, period):
    return value - jnp.floor((value + 0.5) * (1.0 / period)) * period


def iota(shape, dim):
    return lax.broadcasted_iota(jnp.int32, shape, dim)


def halves(x):
    high = x.astype(BF16)
    return high, (x - high.astype(F32)).astype(BF16)


def dot(a, b):
    return jnp.dot(a, b, preferred_element_type=F32)


def dot_rows(a, b):
    return lax.dot_general(a, b, (((1,), (1,)), ((), ())), preferred_element_type=F32)


def kernel(
    volt, steer, chirp, delays, out,
    vbuf, sbuf, cbuf, dbuf, send, recv, w_hi, w_lo, h_hi, h_lo, g_hi, g_lo, gsum,
    acc, last, halo, stat_s, stat_r, spec, xbuf, ybuf, zbuf,
    in_sem, send_sem, recv_sem, halo_sem, stat_ssem, stat_rsem, x_sem, z_sem,
):
    me = lax.axis_index("chan")
    mt = lax.axis_index("tm")
    mx, mz = me // NZ, lax.rem(me, NZ)

    loads = [
        pltpu.make_async_copy(volt.at[:, pl.ds(THIRD[p] * T, T), :], vbuf.at[p], in_sem.at[p])
        for p in range(PARTS)
    ]
    loads += [
        pltpu.make_async_copy(steer.at[0], sbuf, in_sem.at[PARTS]),
        pltpu.make_async_copy(chirp, cbuf, in_sem.at[PARTS + 1]),
        pltpu.make_async_copy(delays, dbuf, in_sem.at[PARTS + 2]),
    ]
    for load in loads:
        load.start()

    barrier = pltpu.get_barrier_semaphore()

    def greet_chan(k, _):
        pl.semaphore_signal(
            barrier, inc=1, device_id={"chan": lax.rem(me + k, NC)}, device_id_type=MESH
        )
        return 0

    def greet_tm(k, _):
        pl.semaphore_signal(
            barrier, inc=1, device_id={"tm": lax.rem(mt + k, NT)}, device_id_type=MESH
        )
        return 0

    lax.fori_loop(1, NC, greet_chan, 0)
    lax.fori_loop(1, NT, greet_tm, 0)

    row, col = iota((2 * CHANNELS, 2 * CHANNELS), 0), iota((2 * CHANNELS, 2 * CHANNELS), 1)
    turns = ((row >> 1) * (col & (CHANNELS - 1))) & (CHANNELS - 1)
    tc, ts = sincos(turns.astype(F32), CHANNELS)
    imag_out, imag_in = (row & 1) == 1, col >= CHANNELS
    table = jnp.where(imag_out == imag_in, tc, jnp.where(imag_out, -ts, ts))
    t_hi, t_lo = halves(table * (1.0 / math.sqrt(CHANNELS)))

    def channelise(p):
        loads[p].wait()
        v_hi, v_lo = halves(vbuf[p].reshape(PER * T, 2 * CHANNELS))
        made = dot_rows(t_hi, v_hi) + dot_rows(t_hi, v_lo) + dot_rows(t_lo, v_hi)
        for s in range(PER):
            send[p, pl.ds(s, 2 * CHANNELS, stride=PER), :] = made[:, s * T : (s + 1) * T]

    def rows_of(c):
        return pl.ds(pl.multiple_of(c * ROWS, ROWS), ROWS)

    def turn(p):
        def one(k, _):
            c = lax.rem(me + k, NC)
            pltpu.make_async_remote_copy(
                src_ref=send.at[p, rows_of(c), :],
                dst_ref=recv.at[p, rows_of(me), :],
                send_sem=send_sem.at[p],
                recv_sem=recv_sem.at[p],
                device_id={"chan": c},
                device_id_type=MESH,
            ).start()
            return 0

        lax.fori_loop(1, NC, one, 0)
        recv[p, rows_of(me), :] = send[p, rows_of(me), :]

    def all_but_own(ref, p):
        return ref.at[p, pl.ds(0, (NC - 1) * ROWS), :]

    with jax.named_scope("channelise"):
        channelise(0)
    with jax.named_scope("greeting"):
        pl.semaphore_wait(barrier, NC - 1 + NT - 1)
    with jax.named_scope("send"):
        turn(0)
        for p in range(1, PARTS):
            channelise(p)
            turn(p)

    with jax.named_scope("steering"):
        loads[PARTS].wait()
        er, ec = iota((STATIONS, 2 * STATIONS), 0), iota((STATIONS, 2 * STATIONS), 1)
        spread = ((ec // ROWS) * PER + (ec & (PER - 1)) == er).astype(F32).astype(BF16)
        rows = 64

        def weigh(j, _):
            at = pl.multiple_of(j * rows, rows)
            index = sbuf[pl.ds(at, rows), :]
            coarse = dot((index >> 5).astype(F32).astype(BF16), spread)
            fine = dot((index & 31).astype(F32).astype(BF16), spread)
            phase = (coarse * 32.0 + fine).astype(jnp.int32)
            column = iota((rows, 2 * STATIONS), 1)
            phase = (phase + ((column >> 3) & 1) * (PHASES // 4)) & (PHASES - 1)
            wc, ws = sincos(phase.astype(F32), PHASES)
            c_hi, c_lo = halves(wc * (1.0 / math.sqrt(STATIONS)))
            s_hi, s_lo = halves(ws * (1.0 / math.sqrt(STATIONS)))
            slab = j // (SB // rows)
            first = pl.multiple_of(lax.rem(j, SB // rows) * rows, rows)
            w_hi[slab, pl.ds(first, rows), :] = c_hi
            w_lo[slab, pl.ds(first, rows), :] = c_lo
            w_hi[slab, pl.ds(SB + first, rows), :] = s_hi
            w_lo[slab, pl.ds(SB + first, rows), :] = s_lo
            return 0

        lax.fori_loop(0, BEAMS // rows, weigh, 0)

    with jax.named_scope("filter"):
        loads[PARTS + 1].wait()
        chirp_row = cbuf[...]
        pair = jnp.where(
            iota((8, WINDOW), 0) == 0,
            jnp.broadcast_to(jnp.cos(chirp_row), (8, WINDOW)),
            jnp.broadcast_to(jnp.sin(chirp_row), (8, WINDOW)),
        )
        turns = (iota((WINDOW, WINDOW), 0) * iota((WINDOW, WINDOW), 1)) & (WINDOW - 1)
        fc, fs = sincos(turns.astype(F32), WINDOW)
        by_cos = jnp.dot(pair, fc, precision=lax.Precision.HIGHEST, preferred_element_type=F32)
        by_sin = jnp.dot(pair, fs, precision=lax.Precision.HIGHEST, preferred_element_type=F32)
        h_re = (by_cos[0:1] - by_sin[1:2]) * (1.0 / WINDOW)
        h_im = (by_sin[0:1] + by_cos[1:2]) * (1.0 / WINDOW)
        for k in range(WINDOW // T):
            def rolled(h):
                full = pltpu.roll(jnp.broadcast_to(h, (T, WINDOW)), k * T, 1, stride=1, stride_axis=0)
                return full[:, HALO:]

            r_hi, r_lo = halves(rolled(h_re))
            i_hi, i_lo = halves(rolled(h_im))
            for ref, re, im in ((h_hi, r_hi, i_hi), (h_lo, r_lo, i_lo)):
                ref[k, 0:T, 0:BLOCK] = re
                ref[k, 0:T, BLOCK:] = im
                ref[k, T:, 0:BLOCK] = -im
                ref[k, T:, BLOCK:] = re

    with jax.named_scope("transform"):
        loads[PARTS + 2].wait()
        own = iota((1, CHANNELS), 1) == me
        delay = jnp.sum(jnp.where(own, dbuf[...], 0).astype(F32), axis=1, keepdims=True)
        shape = (BLOCK, FREQ)
        moved = iota(shape, 0).astype(F32) - delay + BLOCK
        turns = modulo(moved, BLOCK) * (iota(shape, 1) + 1).astype(F32)
        gc, gs = sincos(modulo(turns, BLOCK), BLOCK)
        g = jnp.concatenate([gc, -gs], axis=1) * (1.0 / math.sqrt(BLOCK * CHANNELS))
        gsum[...] = jnp.sum(g, axis=0, keepdims=True)
        g_high, g_low = halves(g)
        g_hi[...] = g_high
        g_lo[...] = g_low

    def form(p):
        r_hi, r_lo = halves(recv[p])
        both = jnp.concatenate([r_hi, r_lo], axis=1)
        for i in range(SLABS):
            wide = dot(w_hi[i], both)
            yield i, wide[:, :T] + wide[:, T:] + dot(w_lo[i], r_hi)

    def convolve(u, k):
        x_hi, x_lo = halves(jnp.concatenate([u[:SB], u[SB:]], axis=1))
        return dot(x_hi, h_hi[k]) + dot(x_lo, h_hi[k]) + dot(x_hi, h_lo[k])

    def arrived(p):
        pltpu.make_async_copy(all_but_own(send, p), all_but_own(recv, p), recv_sem.at[p]).wait()

    with jax.named_scope("wait_part"):
        arrived(0)
    with jax.named_scope("beams"):
        for i, u in form(0):
            last[i] = u
        give = pltpu.make_async_remote_copy(
            src_ref=last,
            dst_ref=halo,
            send_sem=halo_sem.at[0],
            recv_sem=halo_sem.at[1],
            device_id={"tm": lax.rem(mt + 1, NT)},
            device_id_type=MESH,
        )
        give.start()
        for i in range(SLABS):
            acc[i] = convolve(last[i], THIRD[0] + 1)
    with jax.named_scope("wait_part"):
        arrived(1)
    with jax.named_scope("beams"):
        for i, u in form(1):
            acc[i] += convolve(u, THIRD[1] + 1)
        give.wait_recv()
        for i in range(SLABS):
            acc[i] += convolve(jnp.where(mt > 0, halo[i], 0.0), 0)
    with jax.named_scope("wait_part"):
        arrived(2)

    def give_stat(i, k):
        return pltpu.make_async_remote_copy(
            src_ref=stat_s.at[i],
            dst_ref=stat_r.at[i, mt],
            send_sem=stat_ssem.at[i],
            recv_sem=stat_rsem.at[i],
            device_id={"tm": lax.rem(mt + k, NT)},
            device_id_type=MESH,
        )

    with jax.named_scope("detect"):
        for i, u in form(2):
            v = acc[i] + convolve(u, THIRD[2] + 1)
            power = v[:, :BLOCK] * v[:, :BLOCK] + v[:, BLOCK:] * v[:, BLOCK:]
            mean = jnp.sum(power, axis=1, keepdims=True) * (1.0 / BLOCK)
            centred = power - mean
            square = jnp.sum(centred * centred, axis=1, keepdims=True)
            lane = iota((SB, 128), 1)
            stat = jnp.where(lane == 0, mean, jnp.where(lane == 1, square, 0.0))
            stat_s[i] = stat.T[0:8]
            for k in range(1, NT):
                give_stat(i, k).start()
            stat_r[i, mt] = stat_s[i]
            c_hi, c_lo = halves(centred)
            spec[pl.ds(i * SB, SB), :] = dot(c_hi, g_hi[...]) + dot(c_lo, g_hi[...]) + dot(c_hi, g_lo[...])

    xrows = BEAMS // NX
    with jax.named_scope("scale"):
        for i in range(SLABS):
            rest = stat_r.at[i, pl.ds(0, NT - 1)]
            pltpu.make_async_copy(rest, rest, stat_rsem.at[i]).wait()
            total = stat_r[i, 0]
            for j in range(1, NT):
                total = total + stat_r[i, j]
            mean = total[0:1] * (1.0 / NT)
            square = total[1:2]
            for j in range(NT):
                apart = stat_r[i, j][0:1] - mean
                square = square + apart * apart * float(BLOCK)
            scale = lax.rsqrt(square * (1.0 / SPECTRA) + EPSILON)
            shift = stat_s[i][0:1] - mean
            line = iota((128, SB), 0)
            turned = jnp.where(line == 0, scale, jnp.where(line == 1, shift, 0.0)).T
            rows_i = pl.ds(i * SB, SB)
            spec[rows_i, :] = (spec[rows_i, :] + turned[:, 1:2] * gsum[...]) * turned[:, 0:1]
            for x in range(i * SB // xrows, (i + 1) * SB // xrows):
                @pl.when(mx != x)
                def _(x=x):
                    pltpu.make_async_remote_copy(
                        src_ref=spec.at[pl.ds(x * xrows, xrows), :],
                        dst_ref=xbuf.at[mx],
                        send_sem=x_sem.at[0],
                        recv_sem=x_sem.at[1],
                        device_id={"chan": x * NZ + mz},
                        device_id_type=MESH,
                    ).start()

                @pl.when(mx == x)
                def _(x=x):
                    xbuf[x] = spec[pl.ds(x * xrows, xrows), :]

    with jax.named_scope("sum_x"):
        rest_x = xbuf.at[pl.ds(0, NX - 1)]
        pltpu.make_async_copy(rest_x, rest_x, x_sem.at[1]).wait()
        ybuf[...] = (xbuf[0] + xbuf[1]) + (xbuf[2] + xbuf[3])
        share = xrows // NZ

        def hand(k, _):
            z = lax.rem(mz + k, NZ)
            pltpu.make_async_remote_copy(
                src_ref=ybuf.at[pl.ds(pl.multiple_of(z * share, share), share), :],
                dst_ref=zbuf.at[mz],
                send_sem=z_sem.at[0],
                recv_sem=z_sem.at[1],
                device_id={"chan": mx * NZ + z},
                device_id_type=MESH,
            ).start()
            return 0

        lax.fori_loop(1, NZ, hand, 0)
        zbuf[mz] = ybuf[pl.ds(pl.multiple_of(mz * share, share), share), :]
    with jax.named_scope("sum_z"):
        rest_z = zbuf.at[pl.ds(0, NZ - 1)]
        pltpu.make_async_copy(rest_z, rest_z, z_sem.at[1]).wait()
        total = zbuf[0]
        for j in range(1, NZ):
            total = total + zbuf[j]
        out[:, 0, 0, :] = total[:, :FREQ]
        out[:, 0, 1, :] = total[:, FREQ:]

    with jax.named_scope("drain"):
        for p in range(PARTS):
            pltpu.make_async_copy(all_but_own(send, p), all_but_own(send, p), send_sem.at[p]).wait()
        give.wait_send()
        for i in range(SLABS):
            rest = stat_r.at[i, pl.ds(0, NT - 1)]
            pltpu.make_async_copy(rest, rest, stat_ssem.at[i]).wait()
        pltpu.make_async_copy(rest_x, rest_x, x_sem.at[0]).wait()
        pltpu.make_async_copy(rest_z, rest_z, z_sem.at[0]).wait()


def local(voltages, steering, chirp_phase, delays):
    vmem, sem = pltpu.VMEM, pltpu.SemaphoreType.DMA
    return pl.pallas_call(
        kernel,
        out_shape=jax.ShapeDtypeStruct((BEAMS // NC, 1, 2, FREQ), F32),
        in_specs=[pl.BlockSpec(memory_space=pl.ANY)] * 4,
        out_specs=pl.BlockSpec(memory_space=pltpu.VMEM),
        scratch_shapes=[
            vmem((PARTS, PER, T, 2 * CHANNELS), F32),
            vmem((BEAMS, STATIONS), jnp.int32),
            vmem((1, WINDOW), F32),
            vmem((1, CHANNELS), jnp.int32),
            vmem((PARTS, NC * ROWS, T), F32),
            vmem((PARTS, NC * ROWS, T), F32),
            vmem((SLABS, 2 * SB, 2 * STATIONS), BF16),
            vmem((SLABS, 2 * SB, 2 * STATIONS), BF16),
            vmem((WINDOW // T, 2 * T, 2 * BLOCK), BF16),
            vmem((WINDOW // T, 2 * T, 2 * BLOCK), BF16),
            vmem((BLOCK, 2 * FREQ), BF16),
            vmem((BLOCK, 2 * FREQ), BF16),
            vmem((1, 2 * FREQ), F32),
            vmem((SLABS, SB, 2 * BLOCK), F32),
            vmem((SLABS, 2 * SB, T), F32),
            vmem((SLABS, 2 * SB, T), F32),
            vmem((SLABS, 8, SB), F32),
            vmem((SLABS, NT, 8, SB), F32),
            vmem((BEAMS, 2 * FREQ), F32),
            vmem((NX, BEAMS // NX, 2 * FREQ), F32),
            vmem((BEAMS // NX, 2 * FREQ), F32),
            vmem((NZ, BEAMS // NC, 2 * FREQ), F32),
            sem((PARTS + 3,)),
            sem((PARTS,)),
            sem((PARTS,)),
            sem((2,)),
            sem((SLABS,)),
            sem((SLABS,)),
            sem((2,)),
            sem((2,)),
        ],
        compiler_params=pltpu.CompilerParams(
            collective_id=0, has_side_effects=True, vmem_limit_bytes=48 << 20
        ),
    )(voltages, steering, chirp_phase, delays)


def solution(mesh):
    in_specs = (P("chan", "tm", None), P("chan", None, None), P("chan", None), P())
    out_specs = P("chan", None, None, "tm")
    return jax.shard_map(local, mesh=mesh, in_specs=in_specs, out_specs=out_specs, check_vma=False)
```

time: 645 us -> 120 us (0.19); the launches traced: 634 us -> 120 us
  waiting for transfers between devices: 512 us -> 0 us
  Pallas kernels: 0 us -> 115 us
  starting transfers between devices: 29.5 us -> 0 us
  other arithmetic: 26.4 us -> 0 us
  blocking collectives: 25.2 us -> 0 us
  matrix products: 20.4 us -> 0 us
  between operations: 13.6 us -> 0.01 us
    reduce_scatter x1 -> x0, waiting for transfers between devices: 460 us -> none  [local(): lax.psum_scatter(trial_sum(normed, own_delays, block_table, block_len, ch...]
    pallas_call x0 -> x1, Pallas kernels: none -> 115 us  [local(): pl.pallas_call(kernel, out_shape=jax.ShapeDtypeStruct((BEAMS // NC, 1, 2,...]
    all_to_all x1 -> x0, waiting for transfers between devices: 49.6 us -> none  [local(): lax.all_to_all(split, 'chan', split_axis=0, concat_axis=2, tiled=True)]
    psum x2 -> x0, blocking collectives: 25.2 us -> none  [the longest x1 13.2 us: local(): mean_power = lax.psum(jnp.sum(detected, axis=2), 'tm') / spectra_all]
    dot_general x5 -> x0, matrix products: 20.4 us -> none  [the longest x1 6.81 us: dedisperse(): spectrum = jnp.dot(window_flat, forward_table, precision=exact_arithmetic)]
    all_to_all x1 -> x0, starting transfers between devices: 19.2 us -> none  [local(): lax.all_to_all(split, 'chan', split_axis=0, concat_axis=2, tiled=True)]
    sin x5 -> x0, other arithmetic: 14 us -> none  [the longest x3 8.2 us: angle_tables(): return (jnp.cos(angles), jnp.sin(angles))]
    ppermute x1 -> x0, starting transfers between devices: 10.1 us -> none  [from_behind(): lax.ppermute(value, axis, [(source, source + steps) for source in range(i...]
  transfers between devices with their start and end apart: 3 -> 0, of which waited for: 3 -> 0; matrix products, arithmetic and copies ran while one was open for 4% -> 0% of each run, Pallas kernels for 0% -> 0%
where the time goes in v1:
time: 120 us
  Pallas kernels  115 us (96%)
  local copies, waits for them, and re-layouts  4.57 us (4%)
    pallas_call x1, Pallas kernels, local(): pl.pallas_call(kernel, out_shape=jax.ShapeDtypeStruct((BEAMS // NC, 1, 2,...  115 us
    unnamed x9, local copies, waits for them, and re-layouts  4.57 us

profile of v1, /device:TPU:1, one launch (start us, length us, event | category | flops | bytes accessed | tf_op | source)
XLA Modules:
  0.0 120.0 jit_solution(8313774622304877621)
XLA Ops:
  0.0 0.0 copy-start
  0.0 1.4 %copy-done = f32[8,384,128]{2,1,0:T(8,128)S(1)} copy-done((f32[8,384,128]{2,1,0:T(8,128)S(1)}, f32[8,384,128]{2,1,0:T(8,128)}, u32[]{:S(2)}) %copy-start) | copy-done | bytes 1572888
  1.4 0.0 copy-start.1
  1.4 1.2 %copy-done.1 = s32[1,512,512]{2,1,0:T(8,128)S(1)} copy-done((s32[1,512,512]{2,1,0:T(8,128)S(1)}, s32[1,512,512]{2,1,0:T(8,128)}, u32[]{:S(2)}) %copy-start.1) | copy-done | bytes 1048600
  2.6 0.0 copy-start.2
  2.6 0.7 copy-done.2
  3.3 0.0 copy-start.3
  3.3 0.7 copy-done.3
  4.0 115.4 %shard_map.46 = f32[8,1,2,128]{3,2,1,0:T(2,128)S(1)} custom-call(f32[8,384,128]{2,1,0:T(8,128)S(1)} %copy-done, s32[1,512,512]{2,1,0:T(8,128)S(1)} %copy-done.1, f32[1,512]{1,0:T(1,128)S(1)} %copy-done.2, s32[1,64]{1,0:T(1,128)S(1)} %copy-done.3), custom_call_target="tpu_custom_call" | custom-call | tf_op jit(solution)/shard_map/pallas_call | solution.py:367
  119.4 0.6 copy.6
Async XLA Ops:
  0.0 1.4 %copy-start = (f32[8,384,128]{2,1,0:T(8,128)S(1)}, f32[8,384,128]{2,1,0:T(8,128)}, u32[]{:S(2)}) copy-start(f32[8,384,128]{2,1,0:T(8,128)} %volt.1) | copy-start | bytes 4718596
  1.4 1.2 %copy-start.1 = (s32[1,512,512]{2,1,0:T(8,128)S(1)}, s32[1,512,512]{2,1,0:T(8,128)}, u32[]{:S(2)}) copy-start(s32[1,512,512]{2,1,0:T(8,128)} %steer.1) | copy-start | bytes 3145732
  2.6 0.7 copy-start.2
  3.3 0.7 copy-start.3

commit v2 on v1

v2 whole, which is shorter than its diff:
```python
import math

import jax
import jax.numpy as jnp
from jax import lax
from jax.experimental import pallas as pl
from jax.experimental.pallas import tpu as pltpu
from jax.sharding import PartitionSpec as P

MESH = pl.DeviceIdType.MESH
F32 = jnp.float32
BF16 = jnp.bfloat16

NX, NZ, NT = 4, 16, 8
NC = NX * NZ
BEAMS = 512
STATIONS = 512
PER = STATIONS // NC
ROWS = 2 * PER
CHANNELS = 64
BLOCK = 384
HALO = 128
WINDOW = 512
FREQ = 128
PHASES = 1024
SPECTRA = 3072
T = 128
PARTS = BLOCK // T
SLABS = 2
SB = BEAMS // SLABS
XROWS = SB // NX
SHARE = BEAMS // NC
GROUPS = 4
MEMBERS = NC // GROUPS
EPSILON = 1e-06
THIRD = (2, 0, 1)


def shift_of(i):
    j = i >> 2
    half = (j + 1) >> 1
    dz = (NZ // 2 + half * (1 - 2 * (j & 1))) & (NZ - 1)
    return ((i & 3) + 1) & (NX - 1), dz


def sincos(turns, period):
    quarter = ((turns + period / 8) * (4.0 / period)).astype(jnp.int32)
    t = (turns - quarter.astype(F32) * (period / 4)) * (2.0 * math.pi / period)
    t2 = t * t
    s = t * (1.0 + t2 * (-1 / 6 + t2 * (1 / 120 + t2 * (-1 / 5040 + t2 * (1 / 362880)))))
    c = 1.0 + t2 * (-1 / 2 + t2 * (1 / 24 + t2 * (-1 / 720 + t2 * (1 / 40320 - t2 * (1 / 3628800)))))
    odd = (quarter & 1) == 1
    cos_part = jnp.where(odd, s, c)
    sin_part = jnp.where(odd, c, s)
    cos_part = jnp.where(((quarter + 1) & 2) == 2, -cos_part, cos_part)
    sin_part = jnp.where((quarter & 2) == 2, -sin_part, sin_part)
    return cos_part, sin_part


def modulo(value, period):
    return value - jnp.floor((value + 0.5) * (1.0 / period)) * period


def iota(shape, dim):
    return lax.broadcasted_iota(jnp.int32, shape, dim)


def halves(x):
    high = x.astype(BF16)
    return high, (x - high.astype(F32)).astype(BF16)


def dot(a, b):
    return jnp.dot(a, b, preferred_element_type=F32)


def dot_rows(a, b):
    return lax.dot_general(a, b, (((1,), (1,)), ((), ())), preferred_element_type=F32)


def kernel(
    volt, steer, chirp, delays, out,
    vbuf, sbuf, cbuf, dbuf, send, recv, w_hi, w_lo, h_hi, h_lo, g_hi, g_lo, gsum,
    acc, last, halo, beams, stat_s, stat_r, spec, xbuf, ybuf, zbuf,
    in_sem, send_sem, recv_sem, halo_sem, stat_sem, x_ssem, x_rsem, z_sem,
):
    me = lax.axis_index("chan")
    mt = lax.axis_index("tm")
    mx, mz = me // NZ, lax.rem(me, NZ)

    loads = [
        pltpu.make_async_copy(volt.at[:, pl.ds(THIRD[p] * T, T), :], vbuf.at[p], in_sem.at[p])
        for p in range(PARTS)
    ]
    loads += [
        pltpu.make_async_copy(steer.at[0], sbuf, in_sem.at[PARTS]),
        pltpu.make_async_copy(chirp, cbuf, in_sem.at[PARTS + 1]),
        pltpu.make_async_copy(delays, dbuf, in_sem.at[PARTS + 2]),
    ]
    for load in loads:
        load.start()

    barrier = pltpu.get_barrier_semaphore()

    def peer(i):
        dx, dz = shift_of(i)
        return ((mx + dx) & (NX - 1)) * NZ + ((mz + dz) & (NZ - 1))

    def greet_chan(i, _):
        pl.semaphore_signal(barrier, inc=1, device_id={"chan": peer(i)}, device_id_type=MESH)
        return 0

    def relative(i):
        dx, dt = ((i >> 3) + 1) & (NX - 1), ((i & (NT - 1)) + 1) & (NT - 1)
        return ((mx + dx) & (NX - 1)), {
            "chan": ((mx + dx) & (NX - 1)) * NZ + mz,
            "tm": (mt + dt) & (NT - 1),
        }

    def greet_row(i, _):
        @pl.when((i & (NT - 1)) != NT - 1)
        def _():
            pl.semaphore_signal(barrier, inc=1, device_id=relative(i)[1], device_id_type=MESH)

        return 0

    lax.fori_loop(0, NC - 1, greet_chan, 0)
    lax.fori_loop(0, NX * NT - 1, greet_row, 0)

    row, col = iota((2 * CHANNELS, 2 * CHANNELS), 0), iota((2 * CHANNELS, 2 * CHANNELS), 1)
    turns = ((row >> 1) * (col & (CHANNELS - 1))) & (CHANNELS - 1)
    tc, ts = sincos(turns.astype(F32), CHANNELS)
    imag_out, imag_in = (row & 1) == 1, col >= CHANNELS
    table = jnp.where(imag_out == imag_in, tc, jnp.where(imag_out, -ts, ts))
    t_hi, t_lo = halves(table * (1.0 / math.sqrt(CHANNELS)))

    def channelise(p):
        loads[p].wait()
        v_hi, v_lo = halves(vbuf[p].reshape(PER * T, 2 * CHANNELS))
        made = dot_rows(t_hi, v_hi) + dot_rows(t_hi, v_lo) + dot_rows(t_lo, v_hi)
        for s in range(PER):
            send[p, pl.ds(s, 2 * CHANNELS, stride=PER), :] = made[:, s * T : (s + 1) * T]

    def rows_of(c):
        return pl.ds(pl.multiple_of(c * ROWS, ROWS), ROWS)

    def turn(p):
        def one(i, _):
            c = peer(i)
            pltpu.make_async_remote_copy(
                src_ref=send.at[p, rows_of(c), :],
                dst_ref=recv.at[p, rows_of(i), :],
                send_sem=send_sem.at[p],
                recv_sem=recv_sem.at[p, i // MEMBERS],
                device_id={"chan": c},
                device_id_type=MESH,
            ).start()
            return 0

        lax.fori_loop(0, NC - 1, one, 0)
        recv[p, rows_of(NC - 1), :] = send[p, rows_of(me), :]

    def all_but_own(ref, p):
        return ref.at[p, pl.ds(0, (NC - 1) * ROWS), :]

    with jax.named_scope("channelise"):
        channelise(0)
    with jax.named_scope("greeting"):
        pl.semaphore_wait(barrier, NC - 1 + NX * (NT - 1))
    with jax.named_scope("send"):
        turn(0)
        for p in range(1, PARTS):
            channelise(p)
            turn(p)

    with jax.named_scope("steering"):
        loads[PARTS].wait()
        er, ec = iota((STATIONS, 2 * STATIONS), 0), iota((STATIONS, 2 * STATIONS), 1)
        dx, dz = shift_of(ec // ROWS)
        sender = ((mx - dx) & (NX - 1)) * NZ + ((mz - dz) & (NZ - 1))
        spread = (sender * PER + (ec & (PER - 1)) == er).astype(F32).astype(BF16)
        rows = 64

        def weigh(j, _):
            at = pl.multiple_of(j * rows, rows)
            index = sbuf[pl.ds(at, rows), :].reshape(rows // 2 // SHARE, 2, SHARE, STATIONS)
            index = jnp.concatenate(
                [index[:, slab].reshape(rows // 2, STATIONS) for slab in range(SLABS)], axis=0
            )
            coarse = dot((index >> 5).astype(F32).astype(BF16), spread)
            fine = dot((index & 31).astype(F32).astype(BF16), spread)
            phase = (coarse * 32.0 + fine).astype(jnp.int32)
            column = iota((rows, 2 * STATIONS), 1)
            phase = (phase + ((column >> 3) & 1) * (PHASES // 4)) & (PHASES - 1)
            wc, ws = sincos(phase.astype(F32), PHASES)
            c_hi, c_lo = halves(wc * (1.0 / math.sqrt(STATIONS)))
            s_hi, s_lo = halves(ws * (1.0 / math.sqrt(STATIONS)))
            first = pl.multiple_of(j * (rows // 2), rows // 2)
            for slab in range(SLABS):
                part = slice(slab * (rows // 2), (slab + 1) * (rows // 2))
                w_hi[slab, pl.ds(first, rows // 2), :] = c_hi[part]
                w_lo[slab, pl.ds(first, rows // 2), :] = c_lo[part]
                w_hi[slab, pl.ds(SB + first, rows // 2), :] = s_hi[part]
                w_lo[slab, pl.ds(SB + first, rows // 2), :] = s_lo[part]
            return 0

        lax.fori_loop(0, BEAMS // rows, weigh, 0)

    with jax.named_scope("filter"):
        loads[PARTS + 1].wait()
        chirp_row = cbuf[...]
        pair = jnp.where(
            iota((8, WINDOW), 0) == 0,
            jnp.broadcast_to(jnp.cos(chirp_row), (8, WINDOW)),
            jnp.broadcast_to(jnp.sin(chirp_row), (8, WINDOW)),
        )
        turns = (iota((WINDOW, WINDOW), 0) * iota((WINDOW, WINDOW), 1)) & (WINDOW - 1)
        fc, fs = sincos(turns.astype(F32), WINDOW)
        by_cos = jnp.dot(pair, fc, precision=lax.Precision.HIGHEST, preferred_element_type=F32)
        by_sin = jnp.dot(pair, fs, precision=lax.Precision.HIGHEST, preferred_element_type=F32)
        h_re = (by_cos[0:1] - by_sin[1:2]) * (1.0 / WINDOW)
        h_im = (by_sin[0:1] + by_cos[1:2]) * (1.0 / WINDOW)
        for k in range(WINDOW // T):
            def rolled(h):
                full = pltpu.roll(jnp.broadcast_to(h, (T, WINDOW)), k * T, 1, stride=1, stride_axis=0)
                return full[:, HALO:]

            r_hi, r_lo = halves(rolled(h_re))
            i_hi, i_lo = halves(rolled(h_im))
            for ref, re, im in ((h_hi, r_hi, i_hi), (h_lo, r_lo, i_lo)):
                ref[k, 0:T, 0:BLOCK] = re
                ref[k, 0:T, BLOCK:] = im
                ref[k, T:, 0:BLOCK] = -im
                ref[k, T:, BLOCK:] = re

    with jax.named_scope("transform"):
        loads[PARTS + 2].wait()
        own = iota((1, CHANNELS), 1) == me
        delay = jnp.sum(jnp.where(own, dbuf[...], 0).astype(F32), axis=1, keepdims=True)
        shape = (BLOCK, FREQ)
        moved = iota(shape, 0).astype(F32) - delay + BLOCK
        turns = modulo(moved, BLOCK) * (iota(shape, 1) + 1).astype(F32)
        gc, gs = sincos(modulo(turns, BLOCK), BLOCK)
        g = jnp.concatenate([gc, -gs], axis=1) * (1.0 / math.sqrt(BLOCK * CHANNELS))
        gsum[...] = jnp.sum(g, axis=0, keepdims=True)
        g_high, g_low = halves(g)
        g_hi[...] = g_high
        g_lo[...] = g_low

    def form(p, into):
        for g in range(GROUPS):
            size = MEMBERS * ROWS
            there = recv.at[p, pl.ds(g * size, size - ROWS if g == GROUPS - 1 else size), :]
            pltpu.make_async_copy(there, there, recv_sem.at[p, g]).wait()
            columns = pl.ds(g * size, size)
            r_hi, r_lo = halves(recv[p, columns, :])
            both = jnp.concatenate([r_hi, r_lo], axis=1)
            for i in range(SLABS):
                wide = dot(w_hi[i, :, columns], both)
                made = wide[:, :T] + wide[:, T:] + dot(w_lo[i, :, columns], r_hi)
                into[i] = made if g == 0 else into[i] + made

    def convolve(u, k):
        x_hi, x_lo = halves(jnp.concatenate([u[:SB], u[SB:]], axis=1))
        return dot(x_hi, h_hi[k]) + dot(x_lo, h_hi[k]) + dot(x_hi, h_lo[k])

    with jax.named_scope("beams"):
        form(0, last)
        give = pltpu.make_async_remote_copy(
            src_ref=last,
            dst_ref=halo,
            send_sem=halo_sem.at[0],
            recv_sem=halo_sem.at[1],
            device_id={"tm": (mt + 1) & (NT - 1)},
            device_id_type=MESH,
        )
        give.start()
        for i in range(SLABS):
            acc[i] = convolve(last[i], THIRD[0] + 1)
        form(1, beams)
        for i in range(SLABS):
            acc[i] += convolve(beams[i], THIRD[1] + 1)
        give.wait_recv()
        for i in range(SLABS):
            acc[i] += convolve(jnp.where(mt > 0, halo[i], 0.0), 0)
        form(2, beams)

    def stat_tiles(power_stats):
        lane = iota((8, 128), 1)
        for x in range(NX):
            tile = [a[:, x // 2 * 128 : (x // 2 + 1) * 128] for a in power_stats]
            if x % 2 == 0:
                tile[1] = pltpu.roll(tile[1], XROWS, 1)
            else:
                tile[0] = pltpu.roll(tile[0], XROWS, 1)
            stat_s[x, 0:2, :] = jnp.where(lane < XROWS, tile[0], tile[1])[0:2]
            stat_s[x, 2:3, :] = gsum[:, :FREQ]
            stat_s[x, 3:4, :] = gsum[:, FREQ:]

    def hand_x(i):
        for dx in (2, 1, 3):
            x = (mx + dx) & (NX - 1)
            pltpu.make_async_remote_copy(
                src_ref=spec.at[i, pl.ds(pl.multiple_of(x * XROWS, XROWS), XROWS), :],
                dst_ref=xbuf.at[i, mx],
                send_sem=x_ssem.at[i],
                recv_sem=x_rsem.at[i],
                device_id={"chan": x * NZ + mz},
                device_id_type=MESH,
            ).start()

    def detect(i):
        v = acc[i] + convolve(beams[i], THIRD[2] + 1)
        power = v[:, :BLOCK] * v[:, :BLOCK] + v[:, BLOCK:] * v[:, BLOCK:]
        mean = jnp.sum(power, axis=1, keepdims=True) * (1.0 / BLOCK)
        return mean, power - mean

    def transform(i, centred):
        c_hi, c_lo = halves(centred)
        spec[i] = dot(c_hi, g_hi[...]) + dot(c_lo, g_hi[...]) + dot(c_hi, g_lo[...])

    def stat_rows(mean, centred):
        square = jnp.sum(centred * centred, axis=1, keepdims=True)
        lane = iota((SB, 128), 1)
        return jnp.where(lane == 0, mean, jnp.where(lane == 1, square, 0.0)).T[0:8]

    def give_stat(i, _):
        x, device = relative(i)
        pltpu.make_async_remote_copy(
            src_ref=stat_s.at[x],
            dst_ref=stat_r.at[mx * NT + mt],
            send_sem=stat_sem.at[0],
            recv_sem=stat_sem.at[1],
            device_id=device,
            device_id_type=MESH,
        ).start()
        return 0

    with jax.named_scope("detect"):
        mean_0, centred_0 = detect(0)
        transform(0, centred_0)
        hand_x(0)
        mean_1, centred_1 = detect(1)
        stat_tiles([stat_rows(mean_0, centred_0), stat_rows(mean_1, centred_1)])
        lax.fori_loop(0, NX * NT - 1, give_stat, 0)
        transform(1, centred_1)
        hand_x(1)
        stat_r[mx * NT + mt] = stat_s[mx]
        for i in range(SLABS):
            xbuf[i, mx] = spec[i, pl.ds(pl.multiple_of(mx * XROWS, XROWS), XROWS), :]

    with jax.named_scope("drain"):
        for p in range(PARTS):
            pltpu.make_async_copy(all_but_own(send, p), all_but_own(send, p), send_sem.at[p]).wait()
        give.wait_send()

    with jax.named_scope("scale"):
        rest_stat = stat_r.at[pl.ds(0, NX * NT - 1)]
        pltpu.make_async_copy(rest_stat, rest_stat, stat_sem.at[1]).wait()
        line = iota((128, 128), 0)
        lines = jnp.zeros((128, 128), F32)
        sums = []
        for x in range(NX):
            stats = [stat_r[x * NT + j] for j in range(NT)]
            total = stats[0]
            for j in range(1, NT):
                total = total + stats[j]
            mean = total[0:1] * (1.0 / NT)
            square = total[1:2]
            for j in range(NT):
                apart = stats[j][0:1] - mean
                square = square + apart * apart * float(BLOCK)
            scale = lax.rsqrt(square * (1.0 / SPECTRA) + EPSILON)
            own = stat_r[x * NT + mt]
            lines = jnp.where(line == 2 * x, scale, lines)
            lines = jnp.where(line == 2 * x + 1, own[0:1] - mean, lines)
            sums.append(jnp.concatenate([own[2:3], own[3:4]], axis=1))
        turned = lines.T

    with jax.named_scope("sum_x"):
        for i in range(SLABS):
            rest_x = xbuf.at[i, pl.ds(0, NX - 1)]
            pltpu.make_async_copy(rest_x, rest_x, x_rsem.at[i]).wait()
            mine = turned[i * XROWS : (i + 1) * XROWS]
            total = None
            for x in range(NX):
                shift, scale = mine[:, 2 * x + 1 : 2 * x + 2], mine[:, 2 * x : 2 * x + 1]
                term = (xbuf[i, x] + shift * sums[x]) * scale
                total = term if x == 0 else total + term
            ybuf[i] = total
            odd = (mz + i) & 1

            def share_of(z):
                return ybuf.at[i, pl.ds(pl.multiple_of((z >> 1) * SHARE, SHARE), SHARE), :]

            def hand(z):
                pltpu.make_async_remote_copy(
                    src_ref=share_of(z),
                    dst_ref=zbuf.at[mz],
                    send_sem=z_sem.at[0],
                    recv_sem=z_sem.at[1],
                    device_id={"chan": mx * NZ + z},
                    device_id_type=MESH,
                ).start()

            for dz in (8, 6, 10, 4, 12, 2, 14):
                hand((mz + dz + odd) & (NZ - 1))

            @pl.when(odd == 1)
            def _():
                hand((mz + 1) & (NZ - 1))

            @pl.when(odd == 0)
            def _():
                zbuf[mz] = share_of(mz)[...]

    with jax.named_scope("sum_z"):
        rest_z = zbuf.at[pl.ds(0, NZ - 1)]
        pltpu.make_async_copy(rest_z, rest_z, z_sem.at[1]).wait()
        total = zbuf[0]
        for j in range(1, NZ):
            total = total + zbuf[j]
        out[:, 0, 0, :] = total[:, :FREQ]
        out[:, 0, 1, :] = total[:, FREQ:]
        for i in range(SLABS):
            rest_x = xbuf.at[i, pl.ds(0, NX - 1)]
            pltpu.make_async_copy(rest_x, rest_x, x_ssem.at[i]).wait()
        pltpu.make_async_copy(rest_stat, rest_stat, stat_sem.at[0]).wait()
        pltpu.make_async_copy(rest_z, rest_z, z_sem.at[0]).wait()


def local(voltages, steering, chirp_phase, delays):
    vmem, sem = pltpu.VMEM, pltpu.SemaphoreType.DMA
    return pl.pallas_call(
        kernel,
        out_shape=jax.ShapeDtypeStruct((BEAMS // NC, 1, 2, FREQ), F32),
        in_specs=[pl.BlockSpec(memory_space=pltpu.HBM)] * 4,
        out_specs=pl.BlockSpec(memory_space=pltpu.VMEM),
        scratch_shapes=[
            vmem((PARTS, PER, T, 2 * CHANNELS), F32),
            vmem((BEAMS, STATIONS), jnp.int32),
            vmem((1, WINDOW), F32),
            vmem((1, CHANNELS), jnp.int32),
            vmem((PARTS, NC * ROWS, T), F32),
            vmem((PARTS, NC * ROWS, T), F32),
            vmem((SLABS, 2 * SB, 2 * STATIONS), BF16),
            vmem((SLABS, 2 * SB, 2 * STATIONS), BF16),
            vmem((WINDOW // T, 2 * T, 2 * BLOCK), BF16),
            vmem((WINDOW // T, 2 * T, 2 * BLOCK), BF16),
            vmem((BLOCK, 2 * FREQ), BF16),
            vmem((BLOCK, 2 * FREQ), BF16),
            vmem((1, 2 * FREQ), F32),
            vmem((SLABS, SB, 2 * BLOCK), F32),
            vmem((SLABS, 2 * SB, T), F32),
            vmem((SLABS, 2 * SB, T), F32),
            vmem((SLABS, 2 * SB, T), F32),
            vmem((NX, 4, 128), F32),
            vmem((NX * NT, 4, 128), F32),
            vmem((SLABS, SB, 2 * FREQ), F32),
            vmem((SLABS, NX, XROWS, 2 * FREQ), F32),
            vmem((SLABS, XROWS, 2 * FREQ), F32),
            vmem((NZ, SHARE, 2 * FREQ), F32),
            sem((PARTS + 3,)),
            sem((PARTS,)),
            sem((PARTS, GROUPS)),
            sem((2,)),
            sem((2,)),
            sem((SLABS,)),
            sem((SLABS,)),
            sem((2,)),
        ],
        compiler_params=pltpu.CompilerParams(
            collective_id=0, has_side_effects=True, vmem_limit_bytes=64 << 20
        ),
    )(voltages, steering, chirp_phase, delays)


def solution(mesh):
    in_specs = (P("chan", "tm", None), P("chan", None, None), P("chan", None), P())
    out_specs = P("chan", None, None, "tm")
    return jax.shard_map(local, mesh=mesh, in_specs=in_specs, out_specs=out_specs, check_vma=False)
```

time: 120 us -> 109 us (0.908); the launches traced: 120 us -> 107 us
  Pallas kernels: 115 us -> 106 us
  local copies, waits for them, and re-layouts: 4.57 us -> 1.3 us
    pallas_call x1, Pallas kernels: 115 us -> 106 us  [local(): pl.pallas_call(kernel, out_shape=jax.ShapeDtypeStruct((BEAMS // NC, 1, 2,...]
    unnamed x9 -> x1, local copies, waits for them, and re-layouts: 4.57 us -> 1.3 us
where the time goes in v2:
time: 109 us; the launch traced here: 107 us
  Pallas kernels  106 us (97%)
  local copies, waits for them, and re-layouts  1.3 us (1%)
    pallas_call x1, Pallas kernels, local(): pl.pallas_call(kernel, out_shape=jax.ShapeDtypeStruct((BEAMS // NC, 1, 2,...  106 us

profile of v2, /device:TPU:1, one launch (start us, length us, event | category | flops | bytes accessed | tf_op | source)
XLA Modules:
  0.0 107.4 jit_solution(15182008908187532316)
XLA Ops:
  0.0 106.1 %shard_map.46 = f32[8,1,2,128]{3,2,1,0:T(2,128)} custom-call(f32[8,384,128]{2,1,0:T(8,128)} %volt.1, s32[1,512,512]{2,1,0:T(8,128)} %steer.1, f32[1,512]{1,0:T(1,128)} %chirp.1, s32[1,64]{1,0:T(1,128)} %delays.1), custom_call_target="tpu_custom_call" | custom-call | tf_op jit(solution)/shard_map/pallas_call | solution.py:434
  106.1 1.3 %copy.6 = f32[8,1,2,128]{3,2,1,0:T(2,128)} copy(f32[8,1,2,128]{3,2,1,0:T(2,128)} %shard_map.46) | data formatting | bytes 16384

commit v3 on v2

v3 whole, which is shorter than its diff:
```python
import math

import jax
import jax.numpy as jnp
from jax import lax
from jax.experimental import pallas as pl
from jax.experimental.pallas import tpu as pltpu
from jax.sharding import PartitionSpec as P

MESH = pl.DeviceIdType.MESH
F32 = jnp.float32
BF16 = jnp.bfloat16

NX, NZ, NT = 4, 16, 8
NC = NX * NZ
BEAMS = 512
STATIONS = 512
PER = STATIONS // NC
ROWS = 2 * PER
CHANNELS = 64
BLOCK = 384
HALO = 128
WINDOW = 512
FREQ = 128
PHASES = 1024
SPECTRA = 3072
T = 128
PARTS = BLOCK // T
SHARE = BEAMS // NC
OWNERS = ((0, NZ // 4), (NZ // 4, NZ))
SLABS = len(OWNERS)
XROWS = tuple((end - start) * SHARE for start, end in OWNERS)
SIZE = tuple(NX * rows for rows in XROWS)
FIRST = tuple(sum(SIZE[:i]) for i in range(SLABS))
TILES = tuple(size // 128 for size in SIZE)
QUARTER = NZ // 4 * SHARE
GROUPS = 4
REACH = 4
NEAR = NX * (2 * REACH + 1)
MEMBERS = NC // GROUPS
EPSILON = 1e-06
THIRD = (2, 0, 1)


def shift_of(i):
    j = 15 - (i >> 2)
    half = (j + 1) >> 1
    dz = (NZ // 2 + half * (1 - 2 * (j & 1))) & (NZ - 1)
    return i & (NX - 1), dz


def sincos(turns, period):
    quarter = ((turns + period / 8) * (4.0 / period)).astype(jnp.int32)
    t = (turns - quarter.astype(F32) * (period / 4)) * (2.0 * math.pi / period)
    t2 = t * t
    s = t * (1.0 + t2 * (-1 / 6 + t2 * (1 / 120 + t2 * (-1 / 5040 + t2 * (1 / 362880)))))
    c = 1.0 + t2 * (-1 / 2 + t2 * (1 / 24 + t2 * (-1 / 720 + t2 * (1 / 40320 - t2 * (1 / 3628800)))))
    odd = (quarter & 1) == 1
    cos_part = jnp.where(odd, s, c)
    sin_part = jnp.where(odd, c, s)
    cos_part = jnp.where(((quarter + 1) & 2) == 2, -cos_part, cos_part)
    sin_part = jnp.where((quarter & 2) == 2, -sin_part, sin_part)
    return cos_part, sin_part


def modulo(value, period):
    return value - jnp.floor((value + 0.5) * (1.0 / period)) * period


def iota(shape, dim):
    return lax.broadcasted_iota(jnp.int32, shape, dim)


def halves(x):
    high = x.astype(BF16)
    return high, (x - high.astype(F32)).astype(BF16)


def dot(a, b):
    return jnp.dot(a, b, preferred_element_type=F32)


def dot_rows(a, b):
    return lax.dot_general(a, b, (((1,), (1,)), ((), ())), preferred_element_type=F32)


def kernel(
    volt, steer, chirp, delays, zbuf,
    vbuf, sbuf, cbuf, dbuf, send, recv, w_hi, w_lo, h_hi, h_lo, g_hi, g_lo, gsum,
    acc, last, halo, beams, stat_s, stat_r, columns_of, spec, xbuf_0, xbuf_1, ybuf,
    ready, in_sem, send_sem, recv_sem, halo_sem, stat_ssem, stat_rsem, x_ssem, x_rsem, z_sem,
):
    xbuf = (xbuf_0, xbuf_1)
    me = lax.axis_index("chan")
    mt = lax.axis_index("tm")
    mx, mz = me // NZ, lax.rem(me, NZ)

    loads = [
        pltpu.make_async_copy(volt.at[:, pl.ds(THIRD[p] * T, T), :], vbuf.at[p], in_sem.at[p])
        for p in range(PARTS)
    ]
    loads += [
        pltpu.make_async_copy(steer.at[0], sbuf, in_sem.at[PARTS]),
        pltpu.make_async_copy(chirp, cbuf, in_sem.at[PARTS + 1]),
        pltpu.make_async_copy(delays, dbuf, in_sem.at[PARTS + 2]),
    ]
    for load in loads:
        load.start()

    barrier = pltpu.get_barrier_semaphore()

    def peer(i):
        dx, dz = shift_of(i)
        return ((mx + dx) & (NX - 1)) * NZ + ((mz + dz) & (NZ - 1))

    def greet_chan(i, _):
        pl.semaphore_signal(barrier, inc=1, device_id={"chan": peer(i)}, device_id_type=MESH)
        return 0

    def relative(i):
        dx, dt = ((i >> 3) + 1) & (NX - 1), ((i & (NT - 1)) + 1) & (NT - 1)
        return {"chan": ((mx + dx) & (NX - 1)) * NZ + mz, "tm": (mt + dt) & (NT - 1)}

    def greet_row(i, _):
        @pl.when((i & (NT - 1)) != NT - 1)
        def _():
            pl.semaphore_signal(barrier, inc=1, device_id=relative(i), device_id_type=MESH)

        return 0

    lax.fori_loop(1, NEAR, greet_chan, 0)
    lax.fori_loop(0, NX * NT - 1, greet_row, 0)

    row, col = iota((2 * CHANNELS, 2 * CHANNELS), 0), iota((2 * CHANNELS, 2 * CHANNELS), 1)
    turns = ((row >> 1) * (col & (CHANNELS - 1))) & (CHANNELS - 1)
    tc, ts = sincos(turns.astype(F32), CHANNELS)
    imag_out, imag_in = (row & 1) == 1, col >= CHANNELS
    table = jnp.where(imag_out == imag_in, tc, jnp.where(imag_out, -ts, ts))
    t_hi, t_lo = halves(table * (1.0 / math.sqrt(CHANNELS)))

    def channelise(p):
        loads[p].wait()
        v_hi, v_lo = halves(vbuf[p].reshape(PER * T, 2 * CHANNELS))
        made = dot_rows(t_hi, v_hi) + dot_rows(t_hi, v_lo) + dot_rows(t_lo, v_hi)
        for s in range(PER):
            send[p, pl.ds(s, 2 * CHANNELS, stride=PER), :] = made[:, s * T : (s + 1) * T]

    def rows_of(c):
        return pl.ds(pl.multiple_of(c * ROWS, ROWS), ROWS)

    def give(p, i):
        c = peer(i)
        pltpu.make_async_remote_copy(
            src_ref=send.at[p, rows_of(c), :],
            dst_ref=recv.at[p, rows_of(i), :],
            send_sem=send_sem.at[p],
            recv_sem=recv_sem.at[p, i // MEMBERS],
            device_id={"chan": c},
            device_id_type=MESH,
        ).start()

    def turn(p, first, end):
        def one(i, _):
            give(p, i)
            return 0

        lax.fori_loop(first, end, one, 0)

    def turn_back(p):
        def one(i, _):
            give(p, NC - 1 - i)
            return 0

        lax.fori_loop(0, NC - 1, one, 0)

    def all_but_own(ref, p):
        return ref.at[p, pl.ds(0, (NC - 1) * ROWS), :]

    with jax.named_scope("channelise"):
        channelise(0)
    with jax.named_scope("greeting"):
        pl.semaphore_wait(barrier, NEAR - 1 + NX * (NT - 1))
        for dz in (REACH, NZ - REACH):
            pl.semaphore_signal(
                ready,
                inc=1,
                device_id={"chan": mx * NZ + ((mz + dz) & (NZ - 1))},
                device_id_type=MESH,
            )
    with jax.named_scope("send"):
        turn(0, 1, NEAR)
        channelise(1)
        pl.semaphore_wait(ready, 2)
        turn(0, NEAR, NC)
        turn_back(1)
        channelise(2)
        turn_back(2)
        for p in range(PARTS):
            recv[p, rows_of(0), :] = send[p, rows_of(me), :]

    with jax.named_scope("steering"):
        loads[PARTS].wait()
        er, ec = iota((STATIONS, 2 * STATIONS), 0), iota((STATIONS, 2 * STATIONS), 1)
        dx, dz = shift_of(ec // ROWS)
        sender = ((mx - dx) & (NX - 1)) * NZ + ((mz - dz) & (NZ - 1))
        spread = (sender * PER + (ec & (PER - 1)) == er).astype(F32).astype(BF16)
        rows = QUARTER

        def weigh(j, _):
            at = pl.multiple_of(j * rows, rows)
            index = sbuf[pl.ds(at, rows), :]
            coarse = dot((index >> 5).astype(F32).astype(BF16), spread)
            fine = dot((index & 31).astype(F32).astype(BF16), spread)
            phase = (coarse * 32.0 + fine).astype(jnp.int32)
            column = iota((rows, 2 * STATIONS), 1)
            phase = (phase + ((column >> 3) & 1) * (PHASES // 4)) & (PHASES - 1)
            wc, ws = sincos(phase.astype(F32), PHASES)
            c_hi, c_lo = halves(wc * (1.0 / math.sqrt(STATIONS)))
            s_hi, s_lo = halves(ws * (1.0 / math.sqrt(STATIONS)))
            x, quarter = j // 4, j & 3
            early = quarter == 0
            size = jnp.where(early, SIZE[0], SIZE[1])
            first = jnp.where(early, x * XROWS[0], 2 * SIZE[0] + x * XROWS[1] + (quarter - 1) * rows)
            real = pl.ds(pl.multiple_of(first, rows), rows)
            imag = pl.ds(pl.multiple_of(first + size, rows), rows)
            w_hi[real, :] = c_hi
            w_lo[real, :] = c_lo
            w_hi[imag, :] = s_hi
            w_lo[imag, :] = s_lo
            return 0

        lax.fori_loop(0, BEAMS // rows, weigh, 0)

    with jax.named_scope("filter"):
        loads[PARTS + 1].wait()
        chirp_row = cbuf[...]
        pair = jnp.where(
            iota((8, WINDOW), 0) == 0,
            jnp.broadcast_to(jnp.cos(chirp_row), (8, WINDOW)),
            jnp.broadcast_to(jnp.sin(chirp_row), (8, WINDOW)),
        )
        turns = (iota((WINDOW, WINDOW), 0) * iota((WINDOW, WINDOW), 1)) & (WINDOW - 1)
        fc, fs = sincos(turns.astype(F32), WINDOW)
        by_cos = jnp.dot(pair, fc, precision=lax.Precision.HIGHEST, preferred_element_type=F32)
        by_sin = jnp.dot(pair, fs, precision=lax.Precision.HIGHEST, preferred_element_type=F32)
        h_re = (by_cos[0:1] - by_sin[1:2]) * (1.0 / WINDOW)
        h_im = (by_sin[0:1] + by_cos[1:2]) * (1.0 / WINDOW)
        for k in range(WINDOW // T):
            def rolled(h):
                full = pltpu.roll(jnp.broadcast_to(h, (T, WINDOW)), k * T, 1, stride=1, stride_axis=0)
                return full[:, HALO:]

            r_hi, r_lo = halves(rolled(h_re))
            i_hi, i_lo = halves(rolled(h_im))
            for ref, re, im in ((h_hi, r_hi, i_hi), (h_lo, r_lo, i_lo)):
                ref[k, 0:T, 0:BLOCK] = re
                ref[k, 0:T, BLOCK:] = im
                ref[k, T:, 0:BLOCK] = -im
                ref[k, T:, BLOCK:] = re

    with jax.named_scope("transform"):
        loads[PARTS + 2].wait()
        own = iota((1, CHANNELS), 1) == me
        delay = jnp.sum(jnp.where(own, dbuf[...], 0).astype(F32), axis=1, keepdims=True)
        shape = (BLOCK, FREQ)
        moved = iota(shape, 0).astype(F32) - delay + BLOCK
        turns = modulo(moved, BLOCK) * (iota(shape, 1) + 1).astype(F32)
        gc, gs = sincos(modulo(turns, BLOCK), BLOCK)
        g = jnp.concatenate([gc, -gs], axis=1) * (1.0 / math.sqrt(BLOCK * CHANNELS))
        gsum[...] = jnp.sum(g, axis=0, keepdims=True)
        g_high, g_low = halves(g)
        g_hi[...] = g_high
        g_lo[...] = g_low

    def pair_rows(i):
        return pl.ds(2 * FIRST[i], 2 * SIZE[i])

    def slab_rows(i):
        return pl.ds(FIRST[i], SIZE[i])

    def x_rows(i, x):
        return pl.ds(pl.multiple_of(FIRST[i] + x * XROWS[i], SHARE), XROWS[i])

    def form(p, into, groups=tuple(range(GROUPS))[::-1], slabs=range(SLABS)):
        for g in groups:
            size = MEMBERS * ROWS
            if 0 in slabs:
                there = recv.at[p, pl.ds(g * size, size - ROWS if g == 0 else size), :]
                pltpu.make_async_copy(there, there, recv_sem.at[p, g]).wait()
            columns = pl.ds(g * size, size)
            r_hi, r_lo = halves(recv[p, columns, :])
            both = jnp.concatenate([r_hi, r_lo], axis=1)
            for i in slabs:
                wide = dot(w_hi[pair_rows(i), columns], both)
                made = wide[:, :T] + wide[:, T:] + dot(w_lo[pair_rows(i), columns], r_hi)
                into[pair_rows(i), :] = made if g == GROUPS - 1 else into[pair_rows(i), :] + made

    def convolve(u, k, i):
        x_hi, x_lo = halves(jnp.concatenate([u[: SIZE[i]], u[SIZE[i] :]], axis=1))
        return dot(x_hi, h_hi[k]) + dot(x_lo, h_hi[k]) + dot(x_hi, h_lo[k])

    with jax.named_scope("beams"):
        form(0, last)
        halo_copy = pltpu.make_async_remote_copy(
            src_ref=last,
            dst_ref=halo,
            send_sem=halo_sem.at[0],
            recv_sem=halo_sem.at[1],
            device_id={"tm": (mt + 1) & (NT - 1)},
            device_id_type=MESH,
        )
        halo_copy.start()
        for i in range(SLABS):
            acc[slab_rows(i), :] = convolve(last[pair_rows(i), :], THIRD[0] + 1, i)
        form(1, beams)
        for i in range(SLABS):
            acc[slab_rows(i), :] += convolve(beams[pair_rows(i), :], THIRD[1] + 1, i)
        halo_copy.wait_recv()
        for i in range(SLABS):
            acc[slab_rows(i), :] += convolve(jnp.where(mt > 0, halo[pair_rows(i), :], 0.0), 0, i)
        form(2, beams, (3, 2, 1))

    def hand_x(i):
        for dx in (2, 1, 3):
            x = (mx + dx) & (NX - 1)
            pltpu.make_async_remote_copy(
                src_ref=spec.at[x_rows(i, x), :],
                dst_ref=xbuf[i].at[mx],
                send_sem=x_ssem.at[i],
                recv_sem=x_rsem.at[i],
                device_id={"chan": x * NZ + mz},
                device_id_type=MESH,
            ).start()
        xbuf[i][mx] = spec[x_rows(i, mx), :]

    def detect(i):
        v = acc[slab_rows(i), :] + convolve(beams[pair_rows(i), :], THIRD[2] + 1, i)
        power = v[:, :BLOCK] * v[:, :BLOCK] + v[:, BLOCK:] * v[:, BLOCK:]
        mean = jnp.sum(power, axis=1, keepdims=True) * (1.0 / BLOCK)
        centred = power - mean
        square = jnp.sum(centred * centred, axis=1, keepdims=True)
        lane = iota((SIZE[i], 128), 1)
        rows = jnp.where(lane == 0, mean, jnp.where(lane == 1, square, 0.0)).T
        for k in range(TILES[i]):
            stat_s[i, k : k + 1, :] = rows[0:1, k * 128 : (k + 1) * 128]
            stat_s[i, 3 + k : 4 + k, :] = rows[1:2, k * 128 : (k + 1) * 128]
        stat_s[i, 6:7, :] = gsum[:, :FREQ]
        stat_s[i, 7:8, :] = gsum[:, FREQ:]
        return centred

    def transform(i, centred):
        c_hi, c_lo = halves(centred)
        spec[slab_rows(i), :] = dot(c_hi, g_hi[...]) + dot(c_lo, g_hi[...]) + dot(c_hi, g_lo[...])

    def hand_stat(i):
        def one(j, _):
            pltpu.make_async_remote_copy(
                src_ref=stat_s.at[i],
                dst_ref=stat_r.at[i, mx * NT + mt],
                send_sem=stat_ssem.at[i],
                recv_sem=stat_rsem.at[i],
                device_id=relative(j),
                device_id_type=MESH,
            ).start()
            return 0

        lax.fori_loop(0, NX * NT - 1, one, 0)
        stat_r[i, mx * NT + mt] = stat_s[i]

    def rest_stat(i):
        return stat_r.at[i, pl.ds(0, NX * NT - 1)]

    def rest_x(i):
        return xbuf[i].at[pl.ds(0, NX - 1)]

    with jax.named_scope("detect"):
        for i in range(SLABS):
            form(2, beams, (0,), (i,))
            centred = detect(i)
            hand_stat(i)
            transform(i, centred)
            hand_x(i)

    with jax.named_scope("drain"):
        for p in range(PARTS):
            pltpu.make_async_copy(all_but_own(send, p), all_but_own(send, p), send_sem.at[p]).wait()
        halo_copy.wait_send()

    def scale_rows(i):
        pltpu.make_async_copy(rest_stat(i), rest_stat(i), stat_rsem.at[i]).wait()
        n = TILES[i]
        lines = [[] for _ in range(n)]
        sums = []
        for x in range(NX):
            stats = [stat_r[i, x * NT + j] for j in range(NT)]
            total = stats[0]
            for j in range(1, NT):
                total = total + stats[j]
            mean = total[0:n] * (1.0 / NT)
            square = total[3 : 3 + n]
            for j in range(NT):
                apart = stats[j][0:n] - mean
                square = square + apart * apart * float(BLOCK)
            scale = lax.rsqrt(square * (1.0 / SPECTRA) + EPSILON)
            own = stat_r[i, x * NT + mt]
            shift = own[0:n] - mean
            for k in range(n):
                lines[k] += [scale[k : k + 1], shift[k : k + 1]]
            sums.append(jnp.concatenate([own[6:7], own[7:8]], axis=1))
        for k in range(n):
            tile = jnp.concatenate(lines[k] + [jnp.zeros((128 - 2 * NX, 128), F32)], axis=0)
            columns_of[pl.ds(FIRST[i] + k * 128, 128), :] = tile.T
        return sums

    def sum_x(i):
        sums = scale_rows(i)
        pltpu.make_async_copy(rest_x(i), rest_x(i), x_rsem.at[i]).wait()
        mine = columns_of[x_rows(i, mx), :]
        total = None
        for x in range(NX):
            shift, scale = mine[:, 2 * x + 1 : 2 * x + 2], mine[:, 2 * x : 2 * x + 1]
            term = (xbuf[i][x] + shift * sums[x]) * scale
            total = term if x == 0 else total + term
        start, end = OWNERS[i]
        ybuf[pl.ds(start * SHARE, XROWS[i]), 0, 0, :] = total[:, :FREQ]
        ybuf[pl.ds(start * SHARE, XROWS[i]), 0, 1, :] = total[:, FREQ:]

        def one(k, _):
            half = (k + 1) >> 1
            z = (mz + NZ // 2 + half * (1 - 2 * (k & 1))) & (NZ - 1)

            @pl.when((z >= start) & (z < end))
            def _():
                pltpu.make_async_remote_copy(
                    src_ref=ybuf.at[pl.ds(pl.multiple_of(z * SHARE, SHARE), SHARE)],
                    dst_ref=zbuf.at[mz],
                    send_sem=z_sem.at[0],
                    recv_sem=z_sem.at[1],
                    device_id={"chan": mx * NZ + z},
                    device_id_type=MESH,
                ).start()

            return 0

        lax.fori_loop(0, NZ - 1, one, 0)

    with jax.named_scope("sum_x"):
        for i in range(SLABS):
            sum_x(i)
        keep = pltpu.make_async_copy(
            ybuf.at[pl.ds(pl.multiple_of(mz * SHARE, SHARE), SHARE)], zbuf.at[mz], in_sem.at[0]
        )
        keep.start()

    with jax.named_scope("sum_z"):
        rest_z = zbuf.at[pl.ds(0, NZ - 1)]
        pltpu.make_async_copy(rest_z, rest_z, z_sem.at[1]).wait()
        keep.wait()
        for i in range(SLABS):
            pltpu.make_async_copy(rest_x(i), rest_x(i), x_ssem.at[i]).wait()
            pltpu.make_async_copy(rest_stat(i), rest_stat(i), stat_ssem.at[i]).wait()
        pltpu.make_async_copy(rest_z, rest_z, z_sem.at[0]).wait()


def local(voltages, steering, chirp_phase, delays):
    vmem, sem = pltpu.VMEM, pltpu.SemaphoreType.DMA
    terms = pl.pallas_call(
        kernel,
        out_shape=jax.ShapeDtypeStruct((NZ, SHARE, 1, 2, FREQ), F32),
        in_specs=[pl.BlockSpec(memory_space=pltpu.HBM)] * 4,
        out_specs=pl.BlockSpec(memory_space=pltpu.HBM),
        scratch_shapes=[
            vmem((PARTS, PER, T, 2 * CHANNELS), F32),
            vmem((BEAMS, STATIONS), jnp.int32),
            vmem((1, WINDOW), F32),
            vmem((1, CHANNELS), jnp.int32),
            vmem((PARTS, NC * ROWS, T), F32),
            vmem((PARTS, NC * ROWS, T), F32),
            vmem((2 * BEAMS, 2 * STATIONS), BF16),
            vmem((2 * BEAMS, 2 * STATIONS), BF16),
            vmem((WINDOW // T, 2 * T, 2 * BLOCK), BF16),
            vmem((WINDOW // T, 2 * T, 2 * BLOCK), BF16),
            vmem((BLOCK, 2 * FREQ), BF16),
            vmem((BLOCK, 2 * FREQ), BF16),
            vmem((1, 2 * FREQ), F32),
            vmem((BEAMS, 2 * BLOCK), F32),
            vmem((2 * BEAMS, T), F32),
            vmem((2 * BEAMS, T), F32),
            vmem((2 * BEAMS, T), F32),
            vmem((SLABS, 8, 128), F32),
            vmem((SLABS, NX * NT, 8, 128), F32),
            vmem((BEAMS, 128), F32),
            vmem((BEAMS, 2 * FREQ), F32),
            vmem((NX, XROWS[0], 2 * FREQ), F32),
            vmem((NX, XROWS[1], 2 * FREQ), F32),
            vmem((NZ * SHARE, 1, 2, FREQ), F32),
            pltpu.SemaphoreType.REGULAR,
            sem((PARTS + 3,)),
            sem((PARTS,)),
            sem((PARTS, GROUPS)),
            sem((2,)),
            sem((SLABS,)),
            sem((SLABS,)),
            sem((SLABS,)),
            sem((SLABS,)),
            sem((2,)),
        ],
        compiler_params=pltpu.CompilerParams(
            collective_id=0, has_side_effects=True, vmem_limit_bytes=64 << 20
        ),
    )(voltages, steering, chirp_phase, delays)
    return jnp.sum(terms, axis=0)


def solution(mesh):
    in_specs = (P("chan", "tm", None), P("chan", None, None), P("chan", None), P())
    out_specs = P("chan", None, None, "tm")
    return jax.shard_map(local, mesh=mesh, in_specs=in_specs, out_specs=out_specs, check_vma=False)
```

time: 109 us -> 105 us (0.963); the launches traced: 107 us -> 105 us
  Pallas kernels: 106 us -> 104 us
  other arithmetic: 0 us -> 1.55 us
  local copies, waits for them, and re-layouts: 1.3 us -> 0 us
    pallas_call x1, Pallas kernels: 106 us -> 104 us  [local(): pl.pallas_call(kernel, out_shape=jax.ShapeDtypeStruct((NZ, SHARE, 1, 2, F...]
    reduce_sum x0 -> x1, other arithmetic: none -> 1.55 us  [local(): return jnp.sum(terms, axis=0)]
    unnamed x1 -> x0, local copies, waits for them, and re-layouts: 1.3 us -> none
where the time goes in v3:
time: 105 us
  Pallas kernels  104 us (99%)
  other arithmetic  1.55 us (1%)
    pallas_call x1, Pallas kernels, local(): pl.pallas_call(kernel, out_shape=jax.ShapeDtypeStruct((NZ, SHARE, 1, 2, F...  104 us

profile of v3, /device:TPU:1, one launch (start us, length us, event | category | flops | bytes accessed | tf_op | source)
XLA Modules:
  0.0 105.3 jit_solution(8691688114860425022)
XLA Ops:
  0.0 103.7 %shard_map.46 = f32[16,8,1,2,128]{4,3,2,1,0:T(2,128)} custom-call(f32[8,384,128]{2,1,0:T(8,128)} %volt.1, s32[1,512,512]{2,1,0:T(8,128)} %steer.1, f32[1,512]{1,0:T(1,128)} %chirp.1, s32[1,64]{1,0:T(1,128)} %delays.1), custom_call_target="tpu_custom_call" | custom-call | tf_op jit(solution)/shard_map/pallas_call | solution.py:467
  103.7 1.6 %reduce_sum.11 = f32[8,2,128]{2,1,0:T(2,128)} reduce(f32[16,8,1,2,128]{4,3,2,1,0:T(2,128)} %shard_map.46, f32[]{:T(128)} %constant.0.clone.1), dimensions={0,2}, to_apply=%region_0.0 | reduce | flops 30720 | bytes 139268 | tf_op jit(solution)/shard_map/reduce_sum | solution.py:512

commit v4 on v3

--- a/solution.py
+++ b/solution.py
@@ -87,10 +87,11 @@
 def kernel(
     volt, steer, chirp, delays, zbuf,
     vbuf, sbuf, cbuf, dbuf, send, recv, w_hi, w_lo, h_hi, h_lo, g_hi, g_lo, gsum,
-    acc, last, halo, beams, stat_s, stat_r, columns_of, spec, xbuf_0, xbuf_1, ybuf,
+    acc, last, halo, beams, stat_s0, stat_s1, stat_r0, stat_r1, columns_of, spec, xbuf_0, xbuf_1, ybuf,
     ready, in_sem, send_sem, recv_sem, halo_sem, stat_ssem, stat_rsem, x_ssem, x_rsem, z_sem,
 ):
     xbuf = (xbuf_0, xbuf_1)
+    stat_s, stat_r = (stat_s0, stat_s1), (stat_r0, stat_r1)
     me = lax.axis_index("chan")
     mt = lax.axis_index("tm")
     mx, mz = me // NZ, lax.rem(me, NZ)
@@ -341,11 +342,12 @@
         square = jnp.sum(centred * centred, axis=1, keepdims=True)
         lane = iota((SIZE[i], 128), 1)
         rows = jnp.where(lane == 0, mean, jnp.where(lane == 1, square, 0.0)).T
-        for k in range(TILES[i]):
-            stat_s[i, k : k + 1, :] = rows[0:1, k * 128 : (k + 1) * 128]
-            stat_s[i, 3 + k : 4 + k, :] = rows[1:2, k * 128 : (k + 1) * 128]
-        stat_s[i, 6:7, :] = gsum[:, :FREQ]
-        stat_s[i, 7:8, :] = gsum[:, FREQ:]
+        n = TILES[i]
+        for k in range(n):
+            stat_s[i][k : k + 1, :] = rows[0:1, k * 128 : (k + 1) * 128]
+            stat_s[i][n + k : n + k + 1, :] = rows[1:2, k * 128 : (k + 1) * 128]
+        stat_s[i][2 * n : 2 * n + 1, :] = gsum[:, :FREQ]
+        stat_s[i][2 * n + 1 :, :] = gsum[:, FREQ:]
         return centred
 
     def transform(i, centred):
@@ -355,8 +357,8 @@
     def hand_stat(i):
         def one(j, _):
             pltpu.make_async_remote_copy(
-                src_ref=stat_s.at[i],
-                dst_ref=stat_r.at[i, mx * NT + mt],
+                src_ref=stat_s[i],
+                dst_ref=stat_r[i].at[mx * NT + mt],
                 send_sem=stat_ssem.at[i],
                 recv_sem=stat_rsem.at[i],
                 device_id=relative(j),
@@ -365,10 +367,10 @@
             return 0
 
         lax.fori_loop(0, NX * NT - 1, one, 0)
-        stat_r[i, mx * NT + mt] = stat_s[i]
+        stat_r[i][mx * NT + mt] = stat_s[i][...]
 
     def rest_stat(i):
-        return stat_r.at[i, pl.ds(0, NX * NT - 1)]
+        return stat_r[i].at[pl.ds(0, NX * NT - 1)]
 
     def rest_x(i):
         return xbuf[i].at[pl.ds(0, NX - 1)]
@@ -381,32 +383,27 @@
             transform(i, centred)
             hand_x(i)
 
-    with jax.named_scope("drain"):
-        for p in range(PARTS):
-            pltpu.make_async_copy(all_but_own(send, p), all_but_own(send, p), send_sem.at[p]).wait()
-        halo_copy.wait_send()
-
     def scale_rows(i):
         pltpu.make_async_copy(rest_stat(i), rest_stat(i), stat_rsem.at[i]).wait()
         n = TILES[i]
         lines = [[] for _ in range(n)]
         sums = []
         for x in range(NX):
-            stats = [stat_r[i, x * NT + j] for j in range(NT)]
+            stats = [stat_r[i][x * NT + j] for j in range(NT)]
             total = stats[0]
             for j in range(1, NT):
                 total = total + stats[j]
             mean = total[0:n] * (1.0 / NT)
-            square = total[3 : 3 + n]
+            square = total[n : 2 * n]
             for j in range(NT):
                 apart = stats[j][0:n] - mean
                 square = square + apart * apart * float(BLOCK)
             scale = lax.rsqrt(square * (1.0 / SPECTRA) + EPSILON)
-            own = stat_r[i, x * NT + mt]
+            own = stat_r[i][x * NT + mt]
             shift = own[0:n] - mean
             for k in range(n):
                 lines[k] += [scale[k : k + 1], shift[k : k + 1]]
-            sums.append(jnp.concatenate([own[6:7], own[7:8]], axis=1))
+            sums.append(jnp.concatenate([own[2 * n : 2 * n + 1], own[2 * n + 1 :]], axis=1))
         for k in range(n):
             tile = jnp.concatenate(lines[k] + [jnp.zeros((128 - 2 * NX, 128), F32)], axis=0)
             columns_of[pl.ds(FIRST[i] + k * 128, 128), :] = tile.T
@@ -460,6 +457,9 @@
             pltpu.make_async_copy(rest_x(i), rest_x(i), x_ssem.at[i]).wait()
             pltpu.make_async_copy(rest_stat(i), rest_stat(i), stat_ssem.at[i]).wait()
         pltpu.make_async_copy(rest_z, rest_z, z_sem.at[0]).wait()
+        for p in range(PARTS):
+            pltpu.make_async_copy(all_but_own(send, p), all_but_own(send, p), send_sem.at[p]).wait()
+        halo_copy.wait_send()
 
 
 def local(voltages, steering, chirp_phase, delays):
@@ -487,8 +487,10 @@
             vmem((2 * BEAMS, T), F32),
             vmem((2 * BEAMS, T), F32),
             vmem((2 * BEAMS, T), F32),
-            vmem((SLABS, 8, 128), F32),
-            vmem((SLABS, NX * NT, 8, 128), F32),
+            vmem((2 * TILES[0] + 2, 128), F32),
+            vmem((2 * TILES[1] + 2, 128), F32),
+            vmem((NX * NT, 2 * TILES[0] + 2, 128), F32),
+            vmem((NX * NT, 2 * TILES[1] + 2, 128), F32),
             vmem((BEAMS, 128), F32),
             vmem((BEAMS, 2 * FREQ), F32),
             vmem((NX, XROWS[0], 2 * FREQ), F32),

time: 105 us -> 103 us (0.981)
  Pallas kernels: 104 us -> 101 us
    pallas_call x1, Pallas kernels: 104 us -> 101 us  [local(): pl.pallas_call(kernel, out_shape=jax.ShapeDtypeStruct((NZ, SHARE, 1, 2, F...]
where the time goes in v4:
time: 103 us; the launch traced here: 102 us
  Pallas kernels  101 us (98%)
  other arithmetic  1.55 us (2%)
    pallas_call x1, Pallas kernels, local(): pl.pallas_call(kernel, out_shape=jax.ShapeDtypeStruct((NZ, SHARE, 1, 2, F...  101 us

profile of v4, /device:TPU:1, one launch (start us, length us, event | category | flops | bytes accessed | tf_op | source)
XLA Modules:
  0.0 102.4 jit_solution(11237988020485242046)
XLA Ops:
  0.0 100.8 %shard_map.46 = f32[16,8,1,2,128]{4,3,2,1,0:T(2,128)} custom-call(f32[8,384,128]{2,1,0:T(8,128)} %volt.1, s32[1,512,512]{2,1,0:T(8,128)} %steer.1, f32[1,512]{1,0:T(1,128)} %chirp.1, s32[1,64]{1,0:T(1,128)} %delays.1), custom_call_target="tpu_custom_call" | custom-call | tf_op jit(solution)/shard_map/pallas_call | solution.py:467
  100.8 1.6 %reduce_sum.11 = f32[8,2,128]{2,1,0:T(2,128)} reduce(f32[16,8,1,2,128]{4,3,2,1,0:T(2,128)} %shard_map.46, f32[]{:T(128)} %constant.0.clone.1), dimensions={0,2}, to_apply=%region_0.0 | reduce | flops 30720 | bytes 139268 | tf_op jit(solution)/shard_map/reduce_sum | solution.py:514

commit v5 on v4

--- a/solution.py
+++ b/solution.py
@@ -27,7 +27,7 @@
 T = 128
 PARTS = BLOCK // T
 SHARE = BEAMS // NC
-OWNERS = ((0, NZ // 4), (NZ // 4, NZ))
+OWNERS = ((0, NZ // 4), (NZ // 4, NZ // 2), (NZ // 2, NZ))
 SLABS = len(OWNERS)
 XROWS = tuple((end - start) * SHARE for start, end in OWNERS)
 SIZE = tuple(NX * rows for rows in XROWS)
@@ -87,11 +87,11 @@
 def kernel(
     volt, steer, chirp, delays, zbuf,
     vbuf, sbuf, cbuf, dbuf, send, recv, w_hi, w_lo, h_hi, h_lo, g_hi, g_lo, gsum,
-    acc, last, halo, beams, stat_s0, stat_s1, stat_r0, stat_r1, columns_of, spec, xbuf_0, xbuf_1, ybuf,
+    acc, last, halo, beams, stat_s0, stat_s1, stat_s2, stat_r0, stat_r1, stat_r2, columns_of, spec, xbuf_0, xbuf_1, xbuf_2, ybuf,
     ready, in_sem, send_sem, recv_sem, halo_sem, stat_ssem, stat_rsem, x_ssem, x_rsem, z_sem,
 ):
-    xbuf = (xbuf_0, xbuf_1)
-    stat_s, stat_r = (stat_s0, stat_s1), (stat_r0, stat_r1)
+    xbuf = (xbuf_0, xbuf_1, xbuf_2)
+    stat_s, stat_r = (stat_s0, stat_s1, stat_s2), (stat_r0, stat_r1, stat_r2)
     me = lax.axis_index("chan")
     mt = lax.axis_index("tm")
     mx, mz = me // NZ, lax.rem(me, NZ)
@@ -219,9 +219,9 @@
             c_hi, c_lo = halves(wc * (1.0 / math.sqrt(STATIONS)))
             s_hi, s_lo = halves(ws * (1.0 / math.sqrt(STATIONS)))
             x, quarter = j // 4, j & 3
-            early = quarter == 0
-            size = jnp.where(early, SIZE[0], SIZE[1])
-            first = jnp.where(early, x * XROWS[0], 2 * SIZE[0] + x * XROWS[1] + (quarter - 1) * rows)
+            size = jnp.where(quarter < 2, SIZE[0], SIZE[2])
+            late = 2 * FIRST[2] + x * XROWS[2] + (quarter - 2) * rows
+            first = jnp.where(quarter < 2, 2 * FIRST[1] * quarter + x * XROWS[0], late)
             real = pl.ds(pl.multiple_of(first, rows), rows)
             imag = pl.ds(pl.multiple_of(first + size, rows), rows)
             w_hi[real, :] = c_hi
@@ -487,14 +487,11 @@
             vmem((2 * BEAMS, T), F32),
             vmem((2 * BEAMS, T), F32),
             vmem((2 * BEAMS, T), F32),
-            vmem((2 * TILES[0] + 2, 128), F32),
-            vmem((2 * TILES[1] + 2, 128), F32),
-            vmem((NX * NT, 2 * TILES[0] + 2, 128), F32),
-            vmem((NX * NT, 2 * TILES[1] + 2, 128), F32),
+            *[vmem((2 * n + 2, 128), F32) for n in TILES],
+            *[vmem((NX * NT, 2 * n + 2, 128), F32) for n in TILES],
             vmem((BEAMS, 128), F32),
             vmem((BEAMS, 2 * FREQ), F32),
-            vmem((NX, XROWS[0], 2 * FREQ), F32),
-            vmem((NX, XROWS[1], 2 * FREQ), F32),
+            *[vmem((NX, rows, 2 * FREQ), F32) for rows in XROWS],
             vmem((NZ * SHARE, 1, 2, FREQ), F32),
             pltpu.SemaphoreType.REGULAR,
             sem((PARTS + 3,)),

time: 103 us -> 106 us (1.029)
  Pallas kernels: 101 us -> 105 us
    pallas_call x1, Pallas kernels: 101 us -> 105 us  [local(): pl.pallas_call(kernel, out_shape=jax.ShapeDtypeStruct((NZ, SHARE, 1, 2, F...]
where the time goes in v5:
time: 106 us
  Pallas kernels  105 us (99%)
  other arithmetic  1.55 us (1%)
    pallas_call x1, Pallas kernels, local(): pl.pallas_call(kernel, out_shape=jax.ShapeDtypeStruct((NZ, SHARE, 1, 2, F...  105 us

profile of v5, /device:TPU:1, one launch (start us, length us, event | category | flops | bytes accessed | tf_op | source)
XLA Modules:
  0.0 106.2 jit_solution(10346340238988970525)
XLA Ops:
  0.0 104.6 %shard_map.46 = f32[16,8,1,2,128]{4,3,2,1,0:T(2,128)} custom-call(f32[8,384,128]{2,1,0:T(8,128)} %volt.1, s32[1,512,512]{2,1,0:T(8,128)} %steer.1, f32[1,512]{1,0:T(1,128)} %chirp.1, s32[1,64]{1,0:T(1,128)} %delays.1), custom_call_target="tpu_custom_call" | custom-call | tf_op jit(solution)/shard_map/pallas_call | solution.py:467
  104.6 1.6 %reduce_sum.11 = f32[8,2,128]{2,1,0:T(2,128)} reduce(f32[16,8,1,2,128]{4,3,2,1,0:T(2,128)} %shard_map.46, f32[]{:T(128)} %constant.0.clone.1), dimensions={0,2}, to_apply=%region_0.0 | reduce | flops 30720 | bytes 139268 | tf_op jit(solution)/shard_map/reduce_sum | solution.py:511

commit v6 on v4

--- a/solution.py
+++ b/solution.py
@@ -366,7 +366,7 @@
             ).start()
             return 0
 
-        lax.fori_loop(0, NX * NT - 1, one, 0)
+        lax.fori_loop(0, NX * NT - 1, one, 0, unroll=True)
         stat_r[i][mx * NT + mt] = stat_s[i][...]
 
     def rest_stat(i):

time: 103 us -> 103 us (level)
  no operation moved by 1% of the time
where the time goes in v6:
time: 103 us
  Pallas kernels  101 us (98%)
  other arithmetic  1.55 us (2%)
    pallas_call x1, Pallas kernels, local(): pl.pallas_call(kernel, out_shape=jax.ShapeDtypeStruct((NZ, SHARE, 1, 2, F...  101 us

profile of v6, /device:TPU:1, one launch (start us, length us, event | category | flops | bytes accessed | tf_op | source)
XLA Modules:
  0.0 102.7 jit_solution(11727240504797661081)
XLA Ops:
  0.0 101.1 %shard_map.46 = f32[16,8,1,2,128]{4,3,2,1,0:T(2,128)} custom-call(f32[8,384,128]{2,1,0:T(8,128)} %volt.1, s32[1,512,512]{2,1,0:T(8,128)} %steer.1, f32[1,512]{1,0:T(1,128)} %chirp.1, s32[1,64]{1,0:T(1,128)} %delays.1), custom_call_target="tpu_custom_call" | custom-call | tf_op jit(solution)/shard_map/pallas_call | solution.py:467
  101.1 1.6 %reduce_sum.11 = f32[8,2,128]{2,1,0:T(2,128)} reduce(f32[16,8,1,2,128]{4,3,2,1,0:T(2,128)} %shard_map.46, f32[]{:T(128)} %constant.0.clone.1), dimensions={0,2}, to_apply=%region_0.0 | reduce | flops 30720 | bytes 139268 | tf_op jit(solution)/shard_map/reduce_sum | solution.py:514
